TPU v7x, 128 devices: a whole 4x4x4 slice. The times are simulated.
128 devices in a mesh: dp: 8 (over x, z_lo), cent: 16 (over z_hi, y, core).
Axes of the slice: x: 4, y: 4, z: 4 (z_hi: 2, z_lo: 2; z = z_hi * 2 + z_lo), core: 2. Of those that a mesh axis runs over, the one named last changes fastest.
Arguments:
- embeddings: bfloat16 [32768, 1536], P('dp'), may hold values from -20 to 20
- assignments: int32 [32768], P('dp'), may hold values from 0 to 16383, as said below
- parents: bfloat16 [8192, 1536], P('cent'), may hold values from -24 to 24
- starting_coarse_label: int32 [16384], P(('cent', 'dp')), may hold values from 0 to 8191
Outputs:
- centroids: bfloat16 [16384, 1536], P(('cent', 'dp'))
- log_total: float32 [16384], P(('cent', 'dp'))
- parent_mass: float32 [8192], P(('cent', 'dp'))
Inputs may be any that keep to these rules, and one draw needn't show every extreme that they name: `assignments`: split the centroids into aligned runs of 128. Of the rows of one index of dp, at most 48 have their centroid in any one run; one run reaches 48 from every index of dp.
All inputs are finite; a program needn't handle non-finite values.
Results may differ from a plain program's by a relative error of at most 0.0016.
Values may be sent and summed in bfloat16 or wider, within the bound.
A program may use at most 128 MiB of HBM per device.

v0:
```python
import jax
import jax.numpy as jnp
from jax import lax
from jax.sharding import PartitionSpec as P

K1 = 16384


softness_factor = 0.5
retain_coarse_reward = 1.5


def per_device(embeddings, assignments, parents, starting_coarse_label):
    cent_count = lax.axis_size("cent")
    dp_count = lax.axis_size("dp")
    cent_index = lax.axis_index("cent")
    slab = K1 // cent_count
    slab_ids = cent_index * slab + jnp.arange(slab, dtype=jnp.int32)
    onehot = (assignments[:, None] == slab_ids[None, :]).astype(jnp.bfloat16)
    sums = lax.dot_general(
        onehot, embeddings, (((0,), (0,)), ((), ())), preferred_element_type=jnp.float32
    )
    counts = jnp.sum(onehot, axis=0, dtype=jnp.float32)
    sums, counts = (
        lax.psum_scatter(sums, "dp", scatter_dimension=0, tiled=True),
        lax.psum_scatter(counts, "dp", scatter_dimension=0, tiled=True),
    )
    mean = sums / jnp.maximum(counts, 1.0)[:, None]
    scale = jnp.sqrt(jnp.sum(mean * mean, axis=1, keepdims=True) + 1e-06)
    normed = (mean / scale).astype(jnp.bfloat16)
    weight_low = counts.astype(jnp.bfloat16)
    weight = weight_low.astype(jnp.float32)
    piece = lax.all_gather(parents, "cent", axis=0, tiled=True)
    incomplete_affinity_lines = (
        lax.dot_general(normed, piece, (((1,), (1,)), ((), ())), preferred_element_type=jnp.float32)
        / softness_factor
    )
    column_indices = jnp.arange(piece.shape[0], dtype=jnp.int32)
    affinity_grid = incomplete_affinity_lines + retain_coarse_reward * (
        starting_coarse_label[:, None] == column_indices[None, :]
    ).astype(jnp.float32)
    row_top = jnp.max(affinity_grid, axis=1)
    log_total = row_top + jnp.log(jnp.sum(jnp.exp(affinity_grid - row_top[:, None]), axis=1))
    resp = jnp.exp(affinity_grid - log_total[:, None])
    partial_value = jnp.dot(weight, resp, precision=lax.Precision.HIGHEST)
    reordered = partial_value.reshape(cent_count, dp_count, -1).transpose(1, 0, 2).reshape(-1)
    parent_mass = lax.psum_scatter(reordered, ("dp", "cent"), scatter_dimension=0, tiled=True)
    return (normed, log_total, parent_mass)


def solution(mesh):
    return jax.shard_map(
        per_device,
        mesh=mesh,
        in_specs=(P("dp", None), P("dp"), P("cent", None), P(("cent", "dp"))),
        out_specs=(P(("cent", "dp"), None), P(("cent", "dp")), P(("cent", "dp"))),
        check_vma=False,
    )
```

profile of v0, /device:TPU:1, one launch (start us, length us, event | category | flops | bytes accessed | tf_op | source)
XLA Modules:
  0.0 342.0 jit_solution(446222784168201668)
XLA Ops:
  8.0 0.0 reduce-scatter.2.cloned.1.call-start
  8.1 19.3 %fusion = f32[1024,1536]{1,0:T(8,128)} fusion(bf16[4096,1536]{1,0:T(8,128)(2,1)} %param.4, s32[1024]{0:T(1024)S(1)} %iota_add_fusion, s32[4096]{0:T(1024)} %param.5), kind=kOutput, calls=%fused_computation.1 | convolution fusion | flops 12889096192 | bytes 18894848 | tf_op jit(solution)/shard_map/dot_general | solution.py:20
  27.4 0.0 reduce-scatter.2.cloned.1.call-update
  27.4 0.0 all-gather.2.cloned.1.call-start
  27.5 0.5 all-gather.2.cloned.1.call-update
  28.0 0.0 copy-done.5
  28.0 0.6 dynamic-slice
  29.3 2.0 convert_reduce_fusion
  31.2 23.4 %all-reduce = f32[1024]{0:T(1024)S(1)} all-reduce(f32[1024]{0:T(1024)S(1)} %convert_reduce_fusion), channel_id=3, replica_groups=mesh['dp'=8,'cent'=16] {'dp'}, use_global_device_ids=true, to_apply=%region_2.0.clone | all-reduce | flops 1024 | bytes 8192
  54.7 0.1 broadcast_maximum_fusion
  54.8 190.5 %reduce-scatter.2.cloned.1.call-done = f32[128,1536]{1,0:T(8,128)} async-done(((f32[1024,1536]{1,0:T(8,128)}), f32[128,1536]{1,0:T(8,128)}) %reduce-scatter.2.cloned.1.call-update) | async-done | bytes 786448 | tf_op jit(solution)/shard_map/reduce_scatter | solution.py:25
  245.3 1.4 multiply_reduce_fusion
  246.7 0.1 sqrt_multiply_fusion
  246.7 1.3 divide_convert_fusion
  248.0 0.0 copy-start.1
  248.0 0.0 all-gather.2.cloned.1.call-done
  248.1 14.4 %fusion.12 = (f32[128]{0:T(128)S(1)}, f32[128,8192]{1,0:T(8,128)}) fusion(s32[128]{0:T(128)S(1)} %copy-done.4, bf16[128,1536]{1,0:T(8,128)(2,1)S(1)} %divide_convert_fusion, bf16[8192,1536]{1,0:T(8,128)(2,1)} %all-gather.2.cloned.1.call-done), kind=kOutput, calls=%fused_computation.23 | convolution fusion | flops 3226468352 | bytes 29754368 | tf_op jit(solution)/shard_map/dot_general | solution.py:35
  262.5 3.1 exponential_reduce_fusion
  265.6 0.4 copy-done
  265.9 1.9 fusion.5
  267.8 0.1 reshape.32
  267.9 0.1 reshape.33
  268.0 65.9 %all-reduce.1 = f32[8192]{0:T(1024)S(1)} all-reduce(f32[8192]{0:T(1024)S(1)} %reshape.33), channel_id=4, replica_groups=mesh['dp'=8,'cent'=16] {'dp','cent'}, use_global_device_ids=true, to_apply=%region_6.0.clone | all-reduce | flops 8192 | bytes 65536
  333.9 0.6 dynamic-slice.2
  (12 shorter events, 0.0 us)
Async XLA Ops:
  8.0 237.3 %reduce-scatter.2.cloned.1.call-start = ((), (), s32[]{:S(2)}) async-start(), calls=%async_computation.1 | async-start | bytes 7077888 | tf_op jit(solution)/shard_map/reduce_scatter | solution.py:25
  27.4 0.7 copy-start.5
  27.4 1.9 copy-start.3
  27.4 220.7 %copy-start.4 = (s32[128]{0:T(128)S(1)}, s32[128]{0:T(128)}, u32[]{:S(2)}) copy-start(s32[128]{0:T(128)} %param.7) | copy-start | bytes 1540
  27.4 220.6 %all-gather.2.cloned.1.call-start = ((), (), s32[]{:S(2)}) async-start(), calls=%async_computation.2 | async-start | bytes 26738688 | tf_op jit(solution)/shard_map/all_gather | solution.py:33
  248.0 14.5 %copy-start.1 = (bf16[128,1536]{1,0:T(8,128)(2,1)}, bf16[128,1536]{1,0:T(8,128)(2,1)S(1)}, u32[]{:S(2)}) copy-start(bf16[128,1536]{1,0:T(8,128)(2,1)S(1)} %divide_convert_fusion) | copy-start | bytes 1179652
  262.5 3.4 %copy-start = (f32[128,8192]{1,0:T(8,128)S(1)}, f32[128,8192]{1,0:T(8,128)}, u32[]{:S(2)}) copy-start(f32[128,8192]{1,0:T(8,128)} %get-tuple-element.4) | copy-start | bytes 12582916
  265.9 68.6 %copy-start.2 = (f32[128]{0:T(128)}, f32[128]{0:T(128)S(1)}, u32[]{:S(2)}) copy-start(f32[128]{0:T(128)S(1)} %log_add_fusion) | copy-start | bytes 1540
Sparse Core Ops, SparseCore 0:
  27.5 217.7 reduce-scatter.1
Sparse Core Ops, SparseCore 1:
  30.3 185.6 all-gather.1
where the time goes:
time: 342 us
  waiting for transfers between devices  191 us (56%)
  blocking collectives  89.4 us (26%)
  matrix products  35.7 us (10%)
  between operations  16.2 us (5%)
  other arithmetic  7.8 us (2%)
    reduce_scatter x1, waiting for transfers between devices, per_device(): lax.psum_scatter(sums, 'dp', scatter_dimension=0, tiled=True)  191 us
    unnamed x2, blocking collectives  89.4 us
    dot_general x1, matrix products, per_device(): lax.dot_general(onehot, embeddings, (((0,), (0,)), ((), ())), preferred_e...  19.3 us
    dot_general x1, matrix products, per_device(): lax.dot_general(normed, piece, (((1,), (1,)), ((), ())), preferred_elemen...  14.4 us
  transfers between devices with their start and end apart: 2, of which 1 were waited for; matrix products, arithmetic and copies ran while one was open for 2% of the time, Pallas kernels for 0%

commit v1 on v0

v1 whole, which is shorter than its diff:
```python
import jax
import jax.numpy as jnp
from jax import lax
from jax.experimental import pallas as pl
from jax.experimental.pallas import tpu as pltpu
from jax.sharding import PartitionSpec as P

MESH = pl.DeviceIdType.MESH
F32 = jnp.float32
BF16 = jnp.bfloat16

W = 1536
RUN = 128
CAP = 48
DP = 8
SLOTS = DP * CAP
EXT = W + RUN
TILE = 256
NTILE = W // TILE
ROWS = 4096
SLAB = 512
PCH = 256
NPCH = 8
INV_SOFT = 1.0 / 0.5
REWARD = 1.5

RANGES = ((0, 512), (512, 512), (1024, 640))


def kernel(
    a_ref, label_ref, e_hbm, p_hbm,
    cent_ref, logt_ref, mass_ref,
    e_v, oht, bt, slot_v, send, recv, par, cb, meta, scores, mch, sch, stat, fac, mp, sib_in, y_in, ms, mr,
    e_sem, p_sem, row_ss, row_rs, par_ss, par_rs, cb_ss, cb_rs, meta_ss, meta_rs, stat_ss, stat_rs,
    m1_ss, m1_rs, m2_ss, m2_rs,
):
    d = lax.axis_index("dp")
    c = lax.axis_index("cent")
    zlo = d % 2
    zhi = c // 8
    y = (c // 2) % 4
    k = c % 2

    def cent_of(zh, yy, kk):
        return zh * 8 + yy * 2 + kk

    yp, ym, y2 = (y + 1) % 4, (y + 3) % 4, (y + 2) % 4
    flip_d = d - zlo + (1 - zlo)
    group = {
        1: (flip_d, cent_of(1 - zhi, y, k)),
        2: (d, cent_of(zhi, y2, k)),
        3: (flip_d, cent_of(1 - zhi, y2, k)),
    }
    sibling = (d, cent_of(zhi, y, 1 - k))
    up = (d, cent_of(zhi, yp, k))
    down = (d, cent_of(zhi, ym, k))
    up_x = (d, cent_of(zhi, yp, 1 - k))
    down_x = (d, cent_of(zhi, ym, 1 - k))

    def row_peer(r):
        return ((d + r) % DP, c)

    def rcopy(src, dst, ss, rs, dev):
        return pltpu.make_async_remote_copy(
            src_ref=src, dst_ref=dst, send_sem=ss, recv_sem=rs, device_id=dev, device_id_type=MESH
        )

    e_copies = [
        pltpu.make_async_copy(e_hbm.at[:, pl.ds(TILE * n, TILE)], e_v.at[n], e_sem.at[n]) for n in range(NTILE)
    ]
    for cp in e_copies:
        cp.start()
    own_par = pltpu.make_async_copy(p_hbm, par.at[pl.ds(0, SLAB)], p_sem)
    own_par.start()

    barrier = pltpu.get_barrier_semaphore()
    partners = [row_peer(r) for r in range(1, DP)] + [group[1], group[2], group[3], sibling, up, down, up_x, down_x]
    for dev in partners:
        pl.semaphore_signal(barrier, inc=1, device_id=dev, device_id_type=MESH)

    a = a_ref[...]
    rel = lax.shift_right_logical(a, 7) - c * DP
    run_id = lax.broadcasted_iota(jnp.int32, (32, 8, RUN), 1)
    member = (rel[:, None, :] == run_id).astype(F32).reshape(256, RUN)
    member_b = member.astype(BF16)
    upper = (
        lax.broadcasted_iota(jnp.int32, (RUN, RUN), 0) < lax.broadcasted_iota(jnp.int32, (RUN, RUN), 1)
    ).astype(F32).astype(BF16)
    ri = lax.broadcasted_iota(jnp.int32, (256, 256), 0)
    ci = lax.broadcasted_iota(jnp.int32, (256, 256), 1)
    before = (((ri & 7) == (ci & 7)) & (ci < ri)).astype(F32).astype(BF16)
    within = jnp.dot(member_b, upper, preferred_element_type=F32)
    earlier = jnp.dot(before, member_b, preferred_element_type=F32).astype(BF16)
    ahead = jnp.dot(earlier, jnp.ones((RUN, RUN), BF16), preferred_element_type=F32)
    base = ((lax.broadcasted_iota(jnp.int32, (256, RUN), 0) & 7) * CAP + 1).astype(F32)
    slot = jnp.sum((member * (within + ahead + base)).reshape(32, 8, RUN), axis=1) - 1.0
    slot_v[0] = slot.astype(jnp.int32)
    slot_v[1] = a & (RUN - 1)

    pl.semaphore_wait(barrier, len(partners))

    to_up = rcopy(p_hbm.at[pl.ds(0, PCH)], par.at[pl.ds(2 * PCH, PCH)], par_ss.at[0], par_rs.at[0], up)
    to_down = rcopy(p_hbm.at[pl.ds(PCH, PCH)], par.at[pl.ds(3 * PCH, PCH)], par_ss.at[1], par_rs.at[1], down)
    to_sib = rcopy(p_hbm, par.at[pl.ds(4 * PCH, SLAB)], par_ss.at[2], par_rs.at[2], sibling)
    fwd_sib = [
        rcopy(
            par.at[pl.ds((2 + i) * PCH, PCH)], par.at[pl.ds((6 + i) * PCH, PCH)], par_ss.at[3 + i], par_rs.at[3 + i], sibling
        )
        for i in range(2)
    ]
    to_up.start()
    to_down.start()
    to_sib.start()

    def build(b, carry):
        cols = pl.ds(pl.multiple_of(b * RUN, RUN), RUN)
        line = slot_v[0, pl.ds(b, 1), :]
        place = slot_v[1, pl.ds(b, 1), :]
        oht[:, cols] = (lax.broadcasted_iota(jnp.int32, (SLOTS, RUN), 0) == line).astype(F32).astype(BF16)
        bt[:, cols] = (lax.broadcasted_iota(jnp.int32, (RUN, RUN), 0) == place).astype(F32).astype(BF16)
        return carry

    lax.fori_loop(0, ROWS // RUN, build, 0)

    def row_copy(r, g, dev, owner):
        start, size = RANGES[g]
        return rcopy(
            send.at[dev[0], :, pl.ds(start, size)],
            recv.at[owner, :, pl.ds(start, size)],
            row_ss.at[r - 1, g],
            row_rs.at[r - 1, g],
            dev,
        )

    for n in range(NTILE):
        if n == 0:
            ext = lax.dot_general(oht[...], bt[...], (((1,), (1,)), ((), ())), preferred_element_type=F32)
            send[:, :, W:] = ext.astype(BF16).reshape(DP, CAP, RUN)
        e_copies[n].wait()
        part = jnp.dot(oht[...], e_v[n], preferred_element_type=F32)
        send[:, :, TILE * n : TILE * (n + 1)] = part.astype(BF16).reshape(DP, CAP, TILE)
        if n % 2 == 1:
            for r in range(1, DP):
                row_copy(r, n // 2, row_peer(r), d).start()
    recv[d] = send[d]

    for g in range(len(RANGES)):
        for r in range(1, DP):
            row_copy(r, g, row_peer(r), (d + DP - r) % DP).wait_recv()

    got = recv[...].reshape(SLOTS, EXT)
    onehot = got[:, W:]
    sums = lax.dot_general(onehot, got[:, :W], (((0,), (0,)), ((), ())), preferred_element_type=F32)
    counts_col = lax.dot_general(
        onehot, jnp.ones((SLOTS, RUN), BF16), (((0,), (0,)), ((), ())), preferred_element_type=F32
    )[:, :1]
    counts_row = jnp.sum(onehot.astype(F32), axis=0, keepdims=True)
    mean = sums / jnp.maximum(counts_col, 1.0)
    scale = jnp.sqrt(jnp.sum(mean * mean, axis=1, keepdims=True) + 1e-06)
    normed = (mean / scale).astype(BF16)
    cb[0] = normed
    cent_ref[...] = normed
    meta[0, 0:1, :] = counts_row.astype(BF16).astype(F32)
    meta[0, 1:2, :] = label_ref[...].astype(F32)
    meta[0, 2:8, :] = jnp.zeros((6, RUN), F32)

    def half(slot_from, slot_to, h, idx, dev):
        rows = pl.ds(64 * h, 64)
        return rcopy(cb.at[slot_from, rows], cb.at[slot_to, rows], cb_ss.at[idx], cb_rs.at[idx], dev)

    z_first = half(0, 1, 0, 0, group[1])
    z_second = half(0, 1, 1, 1, group[1])
    y_first = half(0, 2, 1, 2, group[2])
    y_second = half(0, 2, 0, 3, group[2])
    fwd_y = half(1, 3, 0, 4, group[2])
    fwd_z = half(2, 3, 1, 5, group[1])
    z_first.start()
    y_first.start()
    metas = {q: rcopy(meta.at[0], meta.at[q], meta_ss.at[q - 1], meta_rs.at[q - 1], group[q]) for q in (1, 2, 3)}
    for q in (1, 2, 3):
        metas[q].start()
    z_second.start()
    y_second.start()

    to_up.wait_recv()
    fwd_sib[0].start()
    to_down.wait_recv()
    fwd_sib[1].start()
    z_first.wait_recv()
    fwd_y.start()
    y_first.wait_recv()
    fwd_z.start()

    own_par.wait()
    to_sib.wait_recv()
    for cp in fwd_sib:
        cp.wait_recv()
    for q in (1, 2, 3):
        metas[q].wait_recv()

    def first_parent(i):
        own, other = k, 1 - k
        lower = cent_of(zhi, ym, 0) * SLAB
        upper_ = cent_of(zhi, yp, 0) * SLAB + PCH
        mine = cent_of(zhi, y, 0) * SLAB
        core = jnp.where(i < 4, own, other) * SLAB
        j = i % 4
        return jnp.where(j < 2, mine + j * PCH, jnp.where(j == 2, lower, upper_)) + core

    def score(pair):
        cols = pl.ds(2 * RUN * pair, 2 * RUN)
        block = cb[2 * pair : 2 * pair + 2].reshape(2 * RUN, W)
        label = jnp.concatenate([meta[2 * pair, 1:2, :], meta[2 * pair + 1, 1:2, :]], axis=1).astype(jnp.int32)

        def step(i, carry):
            s = lax.dot_general(
                par[pl.ds(pl.multiple_of(i * PCH, PCH), PCH), :], block, (((1,), (1,)), ((), ())), preferred_element_type=F32
            )
            ids = lax.broadcasted_iota(jnp.int32, (PCH, 2 * RUN), 0) + first_parent(i)
            s = s * INV_SOFT + jnp.where(ids == label, REWARD, 0.0)
            top = jnp.max(s, axis=0, keepdims=True)
            e = jnp.exp(s - top)
            scores[i, :, cols] = e
            mch[pl.ds(i, 1), cols] = top
            sch[pl.ds(i, 1), cols] = jnp.sum(e, axis=0, keepdims=True)
            return carry

        lax.fori_loop(0, NPCH, step, 0)

    z_second.wait_recv()
    score(0)
    y_second.wait_recv()
    fwd_y.wait_recv()
    fwd_z.wait_recv()
    score(1)

    m_loc = jnp.max(mch[...], axis=0, keepdims=True)
    s_loc = jnp.sum(sch[...] * jnp.exp(mch[...] - m_loc), axis=0, keepdims=True)
    for j in range(4):
        stat[0, j : j + 1, :] = m_loc[:, RUN * j : RUN * (j + 1)]
        stat[0, 4 + j : 5 + j, :] = s_loc[:, RUN * j : RUN * (j + 1)]
    stats = {q: rcopy(stat.at[0], stat.at[q], stat_ss.at[q - 1], stat_rs.at[q - 1], group[q]) for q in (1, 2, 3)}
    for q in (1, 2, 3):
        stats[q].start()
    for q in (1, 2, 3):
        stats[q].wait_recv()
    for j in range(4):
        m = [stat[q, (j ^ q) : (j ^ q) + 1, :] for q in range(4)]
        s = [stat[q, 4 + (j ^ q) : 5 + (j ^ q), :] for q in range(4)]
        top = jnp.maximum(jnp.maximum(m[0], m[1]), jnp.maximum(m[2], m[3]))
        total = sum(s[q] * jnp.exp(m[q] - top) for q in range(4))
        log_total = top + jnp.log(total)
        if j == 0:
            logt_ref[...] = log_total
        cols = slice(RUN * j, RUN * (j + 1))
        fac[:, cols] = meta[j, 0:1, :] * jnp.exp(mch[:, cols] - log_total)

    def mass_step(i, carry):
        f = fac[pl.ds(i, 1), :]
        acc = jnp.zeros((PCH, RUN), F32)
        for j in range(4):
            acc = acc + scores[i, :, RUN * j : RUN * (j + 1)] * f[:, RUN * j : RUN * (j + 1)]
        mp[i] = jnp.sum(acc.T, axis=0, keepdims=True)
        return carry

    lax.fori_loop(0, NPCH, mass_step, 0)

    m1 = [
        rcopy(mp.at[pl.ds(4, 2)], sib_in, m1_ss.at[0], m1_rs.at[0], sibling),
        rcopy(mp.at[2], y_in.at[0], m1_ss.at[1], m1_rs.at[1], down),
        rcopy(mp.at[6], y_in.at[1], m1_ss.at[2], m1_rs.at[2], down_x),
        rcopy(mp.at[3], y_in.at[2], m1_ss.at[3], m1_rs.at[3], up),
        rcopy(mp.at[7], y_in.at[3], m1_ss.at[4], m1_rs.at[4], up_x),
    ]
    for cp in m1:
        cp.start()
    for cp in m1:
        cp.wait_recv()
    halves = (
        mp[0] + sib_in[0] + y_in[0] + y_in[1],
        mp[1] + sib_in[1] + y_in[2] + y_in[3],
    )
    for i in range(DP):
        ms[i, :, :64] = halves[i // 4][:, 64 * (i % 4) : 64 * (i % 4) + 64]
        ms[i, :, 64:] = jnp.zeros((1, 64), F32)
    m2 = []
    for r in range(1, DP):
        dev = row_peer(r)
        cp = rcopy(ms.at[dev[0]], mr.at[d], m2_ss.at[r - 1], m2_rs.at[r - 1], dev)
        cp.start()
    mr[d] = ms[d]
    for r in range(1, DP):
        rcopy(ms.at[row_peer(r)[0]], mr.at[(d + DP - r) % DP], m2_ss.at[r - 1], m2_rs.at[r - 1], row_peer(r)).wait_recv()
    mass_ref[...] = jnp.sum(mr[...], axis=0)[:, :64]

    for cp in [to_up, to_down, to_sib, *fwd_sib, z_first, z_second, y_first, y_second, fwd_y, fwd_z, *m1]:
        cp.wait_send()
    for q in (1, 2, 3):
        metas[q].wait_send()
        stats[q].wait_send()
    for r in range(1, DP):
        for g in range(len(RANGES)):
            row_copy(r, g, row_peer(r), d).wait_send()
        rcopy(ms.at[row_peer(r)[0]], mr.at[d], m2_ss.at[r - 1], m2_rs.at[r - 1], row_peer(r)).wait_send()


def per_device(embeddings, assignments, parents, starting_coarse_label):
    vmem = pl.BlockSpec(memory_space=pltpu.VMEM)
    hbm = pl.BlockSpec(memory_space=pltpu.HBM)
    dma = pltpu.SemaphoreType.DMA
    cent, logt, mass = pl.pallas_call(
        kernel,
        out_shape=(
            jax.ShapeDtypeStruct((RUN, W), BF16),
            jax.ShapeDtypeStruct((1, RUN), F32),
            jax.ShapeDtypeStruct((1, 64), F32),
        ),
        in_specs=[vmem, vmem, hbm, hbm],
        out_specs=(vmem, vmem, vmem),
        scratch_shapes=[
            pltpu.VMEM((NTILE, ROWS, TILE), BF16),
            pltpu.VMEM((SLOTS, ROWS), BF16),
            pltpu.VMEM((RUN, ROWS), BF16),
            pltpu.VMEM((2, 32, RUN), jnp.int32),
            pltpu.VMEM((DP, CAP, EXT), BF16),
            pltpu.VMEM((DP, CAP, EXT), BF16),
            pltpu.VMEM((NPCH * PCH, W), BF16),
            pltpu.VMEM((4, RUN, W), BF16),
            pltpu.VMEM((4, 8, RUN), F32),
            pltpu.VMEM((NPCH, PCH, 4 * RUN), F32),
            pltpu.VMEM((NPCH, 4 * RUN), F32),
            pltpu.VMEM((NPCH, 4 * RUN), F32),
            pltpu.VMEM((4, 8, RUN), F32),
            pltpu.VMEM((NPCH, 4 * RUN), F32),
            pltpu.VMEM((NPCH, 1, PCH), F32),
            pltpu.VMEM((2, 1, PCH), F32),
            pltpu.VMEM((4, 1, PCH), F32),
            pltpu.VMEM((DP, 1, RUN), F32),
            pltpu.VMEM((DP, 1, RUN), F32),
            dma((NTILE,)),
            dma,
            dma((DP - 1, len(RANGES))),
            dma((DP - 1, len(RANGES))),
            dma((5,)),
            dma((5,)),
            dma((6,)),
            dma((6,)),
            dma((3,)),
            dma((3,)),
            dma((3,)),
            dma((3,)),
            dma((5,)),
            dma((5,)),
            dma((DP - 1,)),
            dma((DP - 1,)),
        ],
        compiler_params=pltpu.CompilerParams(collective_id=0, has_side_effects=True, vmem_limit_bytes=56 << 20),
        name="handover",
    )(
        assignments.reshape(32, RUN),
        starting_coarse_label.reshape(1, RUN),
        embeddings,
        parents,
    )
    return cent, logt.reshape(RUN), mass.reshape(64)


def solution(mesh):
    return jax.shard_map(
        per_device,
        mesh=mesh,
        in_specs=(P("dp", None), P("dp"), P("cent", None), P(("cent", "dp"))),
        out_specs=(P(("cent", "dp"), None), P(("cent", "dp")), P(("cent", "dp"))),
        check_vma=False,
    )
```

time: 342 us -> 69.8 us (0.20)
  waiting for transfers between devices: 191 us -> 0 us
  blocking collectives: 89.4 us -> 0 us
  Pallas kernels: 0 us -> 64.8 us
  matrix products: 35.7 us -> 0 us
  between operations: 16.2 us -> 0.64 us
  other arithmetic: 7.8 us -> 0 us
    reduce_scatter x1 -> x0, waiting for transfers between devices: 191 us -> none  [per_device(): lax.psum_scatter(sums, 'dp', scatter_dimension=0, tiled=True)]
    unnamed x2 -> x0, blocking collectives: 89.4 us -> none
    pallas_call x0 -> x1, Pallas kernels: none -> 64.8 us  [per_device(): pl.pallas_call(kernel, out_shape=(jax.ShapeDtypeStruct((RUN, W), BF16), j...]
    dot_general x3 -> x0, matrix products: 35.7 us -> none  [the longest x1 19.3 us: per_device(): lax.dot_general(onehot, embeddings, (((0,), (0,)), ((), ())), preferred_e...]
    reduce_sum x3 -> x0, other arithmetic: 6.37 us -> none  [the longest x1 3.06 us: per_device(): jnp.sum(jnp.exp(affinity_grid - row_top[:, None]), axis=1)]
  transfers between devices with their start and end apart: 2 -> 0, of which waited for: 1 -> 0; matrix products, arithmetic and copies ran while one was open for 2% -> 0% of each run, Pallas kernels for 0% -> 0%
where the time goes in v1:
time: 69.8 us; the launch traced here: 69.6 us
  Pallas kernels  64.8 us (93%)
  local copies, waits for them, and re-layouts  4.08 us (6%)
    pallas_call x1, Pallas kernels, per_device(): pl.pallas_call(kernel, out_shape=(jax.ShapeDtypeStruct((RUN, W), BF16), j...  64.8 us
    unnamed x3, local copies, waits for them, and re-layouts  4.08 us

profile of v1, /device:TPU:1, one launch (start us, length us, event | category | flops | bytes accessed | tf_op | source)
XLA Modules:
  0.0 69.6 jit_solution(13224194191296764287)
XLA Ops:
  0.6 64.8 %handover.1 = (bf16[128,1536]{1,0:T(8,128)(2,1)}, f32[1,128]{1,0:T(1,128)}, f32[1,64]{1,0:T(1,128)}) custom-call(s32[32,128]{1,0:T(8,128)} %bitcast.4, s32[1,128]{1,0:T(1,128)} %bitcast.5, bf16[4096,1536]{1,0:T(8,128)(2,1)} %e_hbm.1, bf16[512,1536]{1,0:T(8,128)(2,1)} %p_hbm.1), custom_call_target="tpu_custom_call" | custom-call | tf_op jit(solution)/shard_map/handover/pallas_call | solution.py:311
  65.5 1.8 %copy.10 = bf16[128,1536]{1,0:T(8,128)(2,1)} copy(bf16[128,1536]{1,0:T(8,128)(2,1)} %get-tuple-element.12) | data formatting | bytes 786432
  67.3 1.1 %copy.11 = f32[128]{0:T(128)} copy(f32[128]{0:T(128)} %bitcast.7) | data formatting | bytes 1024
  68.4 1.2 %copy.12 = f32[64]{0:T(128)} copy(f32[64]{0:T(128)} %bitcast.6) | data formatting | bytes 512

commit v2 on v1

--- a/solution.py
+++ b/solution.py
@@ -17,22 +17,26 @@
 EXT = W + RUN
 TILE = 256
 NTILE = W // TILE
+AHEAD = 2
 ROWS = 4096
 SLAB = 512
-PCH = 256
-NPCH = 8
+PART = 64
+PCH = 512
+NPCH = 4
+HALF = 256
 INV_SOFT = 1.0 / 0.5
 REWARD = 1.5
 
-RANGES = ((0, 512), (512, 512), (1024, 640))
+RANGES = ((0, 256), (256, 512), (768, 896))
+SEND_AFTER = (0, 2, 5)
 
 
 def kernel(
     a_ref, label_ref, e_hbm, p_hbm,
-    cent_ref, logt_ref, mass_ref,
-    e_v, oht, bt, slot_v, send, recv, par, cb, meta, scores, mch, sch, stat, fac, mp, sib_in, y_in, ms, mr,
+    cent_hbm, logt_hbm, mass_hbm,
+    e_v, oht, bt, slot_v, send, recv, par, cb, meta, scores, mch, sch, stat, fac, mp, sib_in, ms, mr, logt_v, mass_v,
     e_sem, p_sem, row_ss, row_rs, par_ss, par_rs, cb_ss, cb_rs, meta_ss, meta_rs, stat_ss, stat_rs,
-    m1_ss, m1_rs, m2_ss, m2_rs,
+    m1_ss, m1_rs, m2_ss, m2_rs, o_sem,
 ):
     d = lax.axis_index("dp")
     c = lax.axis_index("cent")
@@ -54,8 +58,6 @@
     sibling = (d, cent_of(zhi, y, 1 - k))
     up = (d, cent_of(zhi, yp, k))
     down = (d, cent_of(zhi, ym, k))
-    up_x = (d, cent_of(zhi, yp, 1 - k))
-    down_x = (d, cent_of(zhi, ym, 1 - k))
 
     def row_peer(r):
         return ((d + r) % DP, c)
@@ -65,18 +67,19 @@
             src_ref=src, dst_ref=dst, send_sem=ss, recv_sem=rs, device_id=dev, device_id_type=MESH
         )
 
+    barrier = pltpu.get_barrier_semaphore()
+    mass_from = cent_of(zhi, jnp.where(d < 4, yp, ym), k)
+    partners = [row_peer(r) for r in range(1, DP)] + [group[1], group[2], group[3], sibling, up, down]
+    partners += [((d + r) % DP, mass_from) for r in range(DP)]
+    for dev in partners:
+        pl.semaphore_signal(barrier, inc=1, device_id=dev, device_id_type=MESH)
+
     e_copies = [
         pltpu.make_async_copy(e_hbm.at[:, pl.ds(TILE * n, TILE)], e_v.at[n], e_sem.at[n]) for n in range(NTILE)
     ]
-    for cp in e_copies:
+    for cp in e_copies[:AHEAD]:
         cp.start()
     own_par = pltpu.make_async_copy(p_hbm, par.at[pl.ds(0, SLAB)], p_sem)
-    own_par.start()
-
-    barrier = pltpu.get_barrier_semaphore()
-    partners = [row_peer(r) for r in range(1, DP)] + [group[1], group[2], group[3], sibling, up, down, up_x, down_x]
-    for dev in partners:
-        pl.semaphore_signal(barrier, inc=1, device_id=dev, device_id_type=MESH)
 
     a = a_ref[...]
     rel = lax.shift_right_logical(a, 7) - c * DP
@@ -99,18 +102,21 @@
 
     pl.semaphore_wait(barrier, len(partners))
 
-    to_up = rcopy(p_hbm.at[pl.ds(0, PCH)], par.at[pl.ds(2 * PCH, PCH)], par_ss.at[0], par_rs.at[0], up)
-    to_down = rcopy(p_hbm.at[pl.ds(PCH, PCH)], par.at[pl.ds(3 * PCH, PCH)], par_ss.at[1], par_rs.at[1], down)
-    to_sib = rcopy(p_hbm, par.at[pl.ds(4 * PCH, SLAB)], par_ss.at[2], par_rs.at[2], sibling)
+    to_up = rcopy(p_hbm.at[pl.ds(0, HALF)], par.at[pl.ds(SLAB, HALF)], par_ss.at[0], par_rs.at[0], up)
+    to_down = rcopy(p_hbm.at[pl.ds(HALF, HALF)], par.at[pl.ds(SLAB + HALF, HALF)], par_ss.at[1], par_rs.at[1], down)
+    to_sib = rcopy(p_hbm, par.at[pl.ds(2 * SLAB, SLAB)], par_ss.at[2], par_rs.at[2], sibling)
     fwd_sib = [
         rcopy(
-            par.at[pl.ds((2 + i) * PCH, PCH)], par.at[pl.ds((6 + i) * PCH, PCH)], par_ss.at[3 + i], par_rs.at[3 + i], sibling
+            par.at[pl.ds(SLAB + i * HALF, HALF)],
+            par.at[pl.ds(3 * SLAB + i * HALF, HALF)],
+            par_ss.at[3 + i],
+            par_rs.at[3 + i],
+            sibling,
         )
         for i in range(2)
     ]
     to_up.start()
     to_down.start()
-    to_sib.start()
 
     def build(b, carry):
         cols = pl.ds(pl.multiple_of(b * RUN, RUN), RUN)
@@ -133,15 +139,20 @@
         )
 
     for n in range(NTILE):
-        if n == 0:
+        e_copies[n].wait()
+        if n + AHEAD < NTILE:
+            e_copies[n + AHEAD].start()
+        if n == 3:
+            own_par.start()
+            to_sib.start()
+        part = jnp.dot(oht[...], e_v[n], preferred_element_type=F32)
+        send[:, :, TILE * n : TILE * (n + 1)] = part.astype(BF16).reshape(DP, CAP, TILE)
+        if n == NTILE - 1:
             ext = lax.dot_general(oht[...], bt[...], (((1,), (1,)), ((), ())), preferred_element_type=F32)
             send[:, :, W:] = ext.astype(BF16).reshape(DP, CAP, RUN)
-        e_copies[n].wait()
-        part = jnp.dot(oht[...], e_v[n], preferred_element_type=F32)
-        send[:, :, TILE * n : TILE * (n + 1)] = part.astype(BF16).reshape(DP, CAP, TILE)
-        if n % 2 == 1:
+        if n in SEND_AFTER:
             for r in range(1, DP):
-                row_copy(r, n // 2, row_peer(r), d).start()
+                row_copy(r, SEND_AFTER.index(n), row_peer(r), d).start()
     recv[d] = send[d]
 
     for g in range(len(RANGES)):
@@ -159,7 +170,8 @@
     scale = jnp.sqrt(jnp.sum(mean * mean, axis=1, keepdims=True) + 1e-06)
     normed = (mean / scale).astype(BF16)
     cb[0] = normed
-    cent_ref[...] = normed
+    cent_out = pltpu.make_async_copy(cb.at[0], cent_hbm, o_sem.at[0])
+    cent_out.start()
     meta[0, 0:1, :] = counts_row.astype(BF16).astype(F32)
     meta[0, 1:2, :] = label_ref[...].astype(F32)
     meta[0, 2:8, :] = jnp.zeros((6, RUN), F32)
@@ -198,14 +210,12 @@
     for q in (1, 2, 3):
         metas[q].wait_recv()
 
-    def first_parent(i):
-        own, other = k, 1 - k
-        lower = cent_of(zhi, ym, 0) * SLAB
-        upper_ = cent_of(zhi, yp, 0) * SLAB + PCH
-        mine = cent_of(zhi, y, 0) * SLAB
-        core = jnp.where(i < 4, own, other) * SLAB
-        j = i % 4
-        return jnp.where(j < 2, mine + j * PCH, jnp.where(j == 2, lower, upper_)) + core
+    def parent_ids(i):
+        core = jnp.where(i < 2, k, 1 - k)
+        low = cent_of(zhi, jnp.where(i % 2 == 0, y, ym), core) * SLAB
+        high = cent_of(zhi, jnp.where(i % 2 == 0, y, yp), core) * SLAB
+        line = lax.broadcasted_iota(jnp.int32, (PCH, 2 * RUN), 0)
+        return line + jnp.where(line < HALF, low, high)
 
     def score(pair):
         cols = pl.ds(2 * RUN * pair, 2 * RUN)
@@ -216,8 +226,7 @@
             s = lax.dot_general(
                 par[pl.ds(pl.multiple_of(i * PCH, PCH), PCH), :], block, (((1,), (1,)), ((), ())), preferred_element_type=F32
             )
-            ids = lax.broadcasted_iota(jnp.int32, (PCH, 2 * RUN), 0) + first_parent(i)
-            s = s * INV_SOFT + jnp.where(ids == label, REWARD, 0.0)
+            s = s * INV_SOFT + jnp.where(parent_ids(i) == label, REWARD, 0.0)
             top = jnp.max(s, axis=0, keepdims=True)
             e = jnp.exp(s - top)
             scores[i, :, cols] = e
@@ -251,7 +260,9 @@
         total = sum(s[q] * jnp.exp(m[q] - top) for q in range(4))
         log_total = top + jnp.log(total)
         if j == 0:
-            logt_ref[...] = log_total
+            logt_v[...] = log_total
+            logt_out = pltpu.make_async_copy(logt_v, logt_hbm, o_sem.at[1])
+            logt_out.start()
         cols = slice(RUN * j, RUN * (j + 1))
         fac[:, cols] = meta[j, 0:1, :] * jnp.exp(mch[:, cols] - log_total)
 
@@ -265,35 +276,37 @@
 
     lax.fori_loop(0, NPCH, mass_step, 0)
 
-    m1 = [
-        rcopy(mp.at[pl.ds(4, 2)], sib_in, m1_ss.at[0], m1_rs.at[0], sibling),
-        rcopy(mp.at[2], y_in.at[0], m1_ss.at[1], m1_rs.at[1], down),
-        rcopy(mp.at[6], y_in.at[1], m1_ss.at[2], m1_rs.at[2], down_x),
-        rcopy(mp.at[3], y_in.at[2], m1_ss.at[3], m1_rs.at[3], up),
-        rcopy(mp.at[7], y_in.at[3], m1_ss.at[4], m1_rs.at[4], up_x),
-    ]
-    for cp in m1:
-        cp.start()
-    for cp in m1:
-        cp.wait_recv()
-    halves = (
-        mp[0] + sib_in[0] + y_in[0] + y_in[1],
-        mp[1] + sib_in[1] + y_in[2] + y_in[3],
-    )
+    to_sib_mass = rcopy(mp.at[pl.ds(2, 2)], sib_in, m1_ss, m1_rs, sibling)
+    to_sib_mass.start()
+    to_sib_mass.wait_recv()
+    own_slab = mp[0] + sib_in[0]
+    shared = mp[1] + sib_in[1]
     for i in range(DP):
-        ms[i, :, :64] = halves[i // 4][:, 64 * (i % 4) : 64 * (i % 4) + 64]
-        ms[i, :, 64:] = jnp.zeros((1, 64), F32)
+        ms[i, :, :PART] = own_slab[:, PART * i : PART * (i + 1)]
+        ms[i, :, PART:] = jnp.zeros((1, RUN - PART), F32)
+        ms[DP + i, :, :PART] = shared[:, PART * i : PART * (i + 1)]
+        ms[DP + i, :, PART:] = jnp.zeros((1, RUN - PART), F32)
+
     m2 = []
     for r in range(1, DP):
-        dev = row_peer(r)
-        cp = rcopy(ms.at[dev[0]], mr.at[d], m2_ss.at[r - 1], m2_rs.at[r - 1], dev)
+        m2.append(rcopy(ms.at[(d + r) % DP], mr.at[d], m2_ss.at[r - 1], m2_rs.at[d], row_peer(r)))
+    for r in range(4):
+        lo, hi = (d + r) % 4, 4 + (d + r) % 4
+        m2.append(rcopy(ms.at[DP + lo], mr.at[DP + d], m2_ss.at[7 + r], m2_rs.at[DP + d], (lo, cent_of(zhi, ym, k))))
+        m2.append(rcopy(ms.at[DP + hi], mr.at[DP + d], m2_ss.at[11 + r], m2_rs.at[DP + d], (hi, cent_of(zhi, yp, k))))
+    for cp in m2:
         cp.start()
     mr[d] = ms[d]
     for r in range(1, DP):
-        rcopy(ms.at[row_peer(r)[0]], mr.at[(d + DP - r) % DP], m2_ss.at[r - 1], m2_rs.at[r - 1], row_peer(r)).wait_recv()
-    mass_ref[...] = jnp.sum(mr[...], axis=0)[:, :64]
-
-    for cp in [to_up, to_down, to_sib, *fwd_sib, z_first, z_second, y_first, y_second, fwd_y, fwd_z, *m1]:
+        src = (d + r) % DP
+        rcopy(ms.at[0], mr.at[src], m2_ss.at[0], m2_rs.at[src], row_peer(r)).wait_recv()
+    for r in range(DP):
+        rcopy(ms.at[0], mr.at[DP + r], m2_ss.at[0], m2_rs.at[DP + r], row_peer(1)).wait_recv()
+    mass_v[...] = jnp.sum(mr[...], axis=0)[:, :PART]
+    mass_out = pltpu.make_async_copy(mass_v, mass_hbm, o_sem.at[2])
+    mass_out.start()
+
+    for cp in [to_up, to_down, to_sib, *fwd_sib, z_first, z_second, y_first, y_second, fwd_y, fwd_z, to_sib_mass, *m2]:
         cp.wait_send()
     for q in (1, 2, 3):
         metas[q].wait_send()
@@ -301,7 +314,18 @@
     for r in range(1, DP):
         for g in range(len(RANGES)):
             row_copy(r, g, row_peer(r), d).wait_send()
-        rcopy(ms.at[row_peer(r)[0]], mr.at[d], m2_ss.at[r - 1], m2_rs.at[r - 1], row_peer(r)).wait_send()
+    cent_out.wait()
+    logt_out.wait()
+    mass_out.wait()
+
+
+def hand_on(cent, logt, mass, cent_out, logt_out, mass_out, sem):
+    pairs = ((cent, cent_out), (logt, logt_out), (mass, mass_out))
+    copies = [pltpu.make_async_copy(src, dst, sem.at[i]) for i, (src, dst) in enumerate(pairs)]
+    for cp in copies:
+        cp.start()
+    for cp in copies:
+        cp.wait()
 
 
 def per_device(embeddings, assignments, parents, starting_coarse_label):
@@ -313,10 +337,10 @@
         out_shape=(
             jax.ShapeDtypeStruct((RUN, W), BF16),
             jax.ShapeDtypeStruct((1, RUN), F32),
-            jax.ShapeDtypeStruct((1, 64), F32),
+            jax.ShapeDtypeStruct((1, PART), F32),
         ),
         in_specs=[vmem, vmem, hbm, hbm],
-        out_specs=(vmem, vmem, vmem),
+        out_specs=(hbm, hbm, hbm),
         scratch_shapes=[
             pltpu.VMEM((NTILE, ROWS, TILE), BF16),
             pltpu.VMEM((SLOTS, ROWS), BF16),
@@ -334,9 +358,10 @@
             pltpu.VMEM((NPCH, 4 * RUN), F32),
             pltpu.VMEM((NPCH, 1, PCH), F32),
             pltpu.VMEM((2, 1, PCH), F32),
-            pltpu.VMEM((4, 1, PCH), F32),
-            pltpu.VMEM((DP, 1, RUN), F32),
-            pltpu.VMEM((DP, 1, RUN), F32),
+            pltpu.VMEM((2 * DP, 1, RUN), F32),
+            pltpu.VMEM((2 * DP, 1, RUN), F32),
+            pltpu.VMEM((1, RUN), F32),
+            pltpu.VMEM((1, PART), F32),
             dma((NTILE,)),
             dma,
             dma((DP - 1, len(RANGES))),
@@ -349,10 +374,11 @@
             dma((3,)),
             dma((3,)),
             dma((3,)),
-            dma((5,)),
-            dma((5,)),
-            dma((DP - 1,)),
-            dma((DP - 1,)),
+            dma,
+            dma,
+            dma((2 * DP - 1,)),
+            dma((2 * DP,)),
+            dma((3,)),
         ],
         compiler_params=pltpu.CompilerParams(collective_id=0, has_side_effects=True, vmem_limit_bytes=56 << 20),
         name="handover",
@@ -362,7 +388,15 @@
         embeddings,
         parents,
     )
-    return cent, logt.reshape(RUN), mass.reshape(64)
+    cent, logt, mass = pl.pallas_call(
+        hand_on,
+        out_shape=tuple(jax.ShapeDtypeStruct(v.shape, v.dtype) for v in (cent, logt, mass)),
+        in_specs=[hbm, hbm, hbm],
+        out_specs=(hbm, hbm, hbm),
+        scratch_shapes=[dma((3,))],
+        name="finish",
+    )(cent, logt, mass)
+    return cent, logt.reshape(RUN), mass.reshape(PART)
 
 
 def solution(mesh):

time: 69.8 us -> 74.6 us (1.069)
  Pallas kernels: 64.8 us -> 73.8 us
  local copies, waits for them, and re-layouts: 4.08 us -> 0 us
    pallas_call x0 -> x1, Pallas kernels: none -> 13.1 us  [per_device(): pl.pallas_call(hand_on, out_shape=tuple((jax.ShapeDtypeStruct(v.shape, v....]
    pallas_call x1, Pallas kernels: 64.8 us -> 60.7 us  [per_device(): pl.pallas_call(kernel, out_shape=(jax.ShapeDtypeStruct((RUN, W), BF16), j...]
    unnamed x3 -> x0, local copies, waits for them, and re-layouts: 4.08 us -> none
where the time goes in v2:
time: 74.6 us; the launch traced here: 74.4 us
  Pallas kernels  73.8 us (99%)
    pallas_call x1, Pallas kernels, per_device(): pl.pallas_call(kernel, out_shape=(jax.ShapeDtypeStruct((RUN, W), BF16), j...  60.7 us
    pallas_call x1, Pallas kernels, per_device(): pl.pallas_call(hand_on, out_shape=tuple((jax.ShapeDtypeStruct(v.shape, v....  13.1 us

profile of v2, /device:TPU:1, one launch (start us, length us, event | category | flops | bytes accessed | tf_op | source)
XLA Modules:
  0.0 74.4 jit_solution(2536171011076573347)
XLA Ops:
  0.6 60.7 %handover.1 = (bf16[128,1536]{1,0:T(8,128)(2,1)}, f32[1,128]{1,0:T(1,128)}, f32[1,64]{1,0:T(1,128)}) custom-call(s32[32,128]{1,0:T(8,128)} %bitcast.4, s32[1,128]{1,0:T(1,128)} %bitcast.5, bf16[4096,1536]{1,0:T(8,128)(2,1)} %e_hbm.1, bf16[512,1536]{1,0:T(8,128)(2,1)} %p_hbm.1), custom_call_target="tpu_custom_call" | custom-call | tf_op jit(solution)/shard_map/handover/pallas_call | solution.py:335
  61.4 13.1 %finish.1 = (bf16[128,1536]{1,0:T(8,128)(2,1)}, f32[1,128]{1,0:T(1,128)}, f32[1,64]{1,0:T(1,128)}) custom-call(bf16[128,1536]{1,0:T(8,128)(2,1)} %get-tuple-element.9.cent, f32[1,128]{1,0:T(1,128)} %get-tuple-element.10.logt, f32[1,64]{1,0:T(1,128)} %get-tuple-element.11.mass), custom_call_target="tpu_custom_call" | custom-call | tf_op jit(solution)/shard_map/finish/pallas_call | solution.py:391

commit v3 on v2

--- a/solution.py
+++ b/solution.py
@@ -21,8 +21,8 @@
 ROWS = 4096
 SLAB = 512
 PART = 64
-PCH = 512
-NPCH = 4
+PCH = 1024
+NPCH = 2
 HALF = 256
 INV_SOFT = 1.0 / 0.5
 REWARD = 1.5
@@ -100,6 +100,8 @@
     slot_v[0] = slot.astype(jnp.int32)
     slot_v[1] = a & (RUN - 1)
 
+    for cp in e_copies[AHEAD : 2 * AHEAD]:
+        cp.start()
     pl.semaphore_wait(barrier, len(partners))
 
     to_up = rcopy(p_hbm.at[pl.ds(0, HALF)], par.at[pl.ds(SLAB, HALF)], par_ss.at[0], par_rs.at[0], up)
@@ -118,6 +120,9 @@
     to_up.start()
     to_down.start()
 
+    for cp in e_copies[2 * AHEAD :]:
+        cp.start()
+
     def build(b, carry):
         cols = pl.ds(pl.multiple_of(b * RUN, RUN), RUN)
         line = slot_v[0, pl.ds(b, 1), :]
@@ -140,9 +145,7 @@
 
     for n in range(NTILE):
         e_copies[n].wait()
-        if n + AHEAD < NTILE:
-            e_copies[n + AHEAD].start()
-        if n == 3:
+        if n == 2:
             own_par.start()
             to_sib.start()
         part = jnp.dot(oht[...], e_v[n], preferred_element_type=F32)
@@ -154,6 +157,8 @@
             for r in range(1, DP):
                 row_copy(r, SEND_AFTER.index(n), row_peer(r), d).start()
     recv[d] = send[d]
+
+    ms[...] = jnp.zeros_like(ms)
 
     for g in range(len(RANGES)):
         for r in range(1, DP):
@@ -194,6 +199,9 @@
     z_second.start()
     y_second.start()
 
+    for r in range(1, DP):
+        for g in range(len(RANGES)):
+            row_copy(r, g, row_peer(r), d).wait_send()
     to_up.wait_recv()
     fwd_sib[0].start()
     to_down.wait_recv()
@@ -211,11 +219,10 @@
         metas[q].wait_recv()
 
     def parent_ids(i):
-        core = jnp.where(i < 2, k, 1 - k)
-        low = cent_of(zhi, jnp.where(i % 2 == 0, y, ym), core) * SLAB
-        high = cent_of(zhi, jnp.where(i % 2 == 0, y, yp), core) * SLAB
+        core = jnp.where(i == 0, k, 1 - k)
+        mine, low, high = (cent_of(zhi, v, core) * SLAB for v in (y, ym, yp))
         line = lax.broadcasted_iota(jnp.int32, (PCH, 2 * RUN), 0)
-        return line + jnp.where(line < HALF, low, high)
+        return (line & (SLAB - 1)) + jnp.where(line < SLAB, mine, jnp.where(line < SLAB + HALF, low, high))
 
     def score(pair):
         cols = pl.ds(2 * RUN * pair, 2 * RUN)
@@ -238,6 +245,9 @@
 
     z_second.wait_recv()
     score(0)
+    for cp in [to_up, to_down, to_sib, *fwd_sib, *metas.values(), z_first, z_second, y_first]:
+        cp.wait_send()
+    cent_out.wait()
     y_second.wait_recv()
     fwd_y.wait_recv()
     fwd_z.wait_recv()
@@ -251,6 +261,8 @@
     stats = {q: rcopy(stat.at[0], stat.at[q], stat_ss.at[q - 1], stat_rs.at[q - 1], group[q]) for q in (1, 2, 3)}
     for q in (1, 2, 3):
         stats[q].start()
+    for cp in [y_second, fwd_y, fwd_z]:
+        cp.wait_send()
     for q in (1, 2, 3):
         stats[q].wait_recv()
     for j in range(4):
@@ -276,16 +288,12 @@
 
     lax.fori_loop(0, NPCH, mass_step, 0)
 
-    to_sib_mass = rcopy(mp.at[pl.ds(2, 2)], sib_in, m1_ss, m1_rs, sibling)
+    to_sib_mass = rcopy(mp.at[1], sib_in, m1_ss, m1_rs, sibling)
     to_sib_mass.start()
     to_sib_mass.wait_recv()
-    own_slab = mp[0] + sib_in[0]
-    shared = mp[1] + sib_in[1]
-    for i in range(DP):
-        ms[i, :, :PART] = own_slab[:, PART * i : PART * (i + 1)]
-        ms[i, :, PART:] = jnp.zeros((1, RUN - PART), F32)
-        ms[DP + i, :, :PART] = shared[:, PART * i : PART * (i + 1)]
-        ms[DP + i, :, PART:] = jnp.zeros((1, RUN - PART), F32)
+    both = mp[0] + sib_in[...]
+    for i in range(2 * DP):
+        ms[i, :, :PART] = both[:, PART * i : PART * (i + 1)]
 
     m2 = []
     for r in range(1, DP):
@@ -306,26 +314,16 @@
     mass_out = pltpu.make_async_copy(mass_v, mass_hbm, o_sem.at[2])
     mass_out.start()
 
-    for cp in [to_up, to_down, to_sib, *fwd_sib, z_first, z_second, y_first, y_second, fwd_y, fwd_z, to_sib_mass, *m2]:
+    for cp in [to_sib_mass, *stats.values(), *m2]:
         cp.wait_send()
-    for q in (1, 2, 3):
-        metas[q].wait_send()
-        stats[q].wait_send()
-    for r in range(1, DP):
-        for g in range(len(RANGES)):
-            row_copy(r, g, row_peer(r), d).wait_send()
-    cent_out.wait()
     logt_out.wait()
     mass_out.wait()
 
 
-def hand_on(cent, logt, mass, cent_out, logt_out, mass_out, sem):
-    pairs = ((cent, cent_out), (logt, logt_out), (mass, mass_out))
-    copies = [pltpu.make_async_copy(src, dst, sem.at[i]) for i, (src, dst) in enumerate(pairs)]
-    for cp in copies:
-        cp.start()
-    for cp in copies:
-        cp.wait()
+def hand_on(cent, logt, mass, cent_out, logt_out, mass_out):
+    cent_out[...] = cent[...]
+    logt_out[...] = logt[...]
+    mass_out[...] = mass[...]
 
 
 def per_device(embeddings, assignments, parents, starting_coarse_label):
@@ -357,7 +355,7 @@
             pltpu.VMEM((4, 8, RUN), F32),
             pltpu.VMEM((NPCH, 4 * RUN), F32),
             pltpu.VMEM((NPCH, 1, PCH), F32),
-            pltpu.VMEM((2, 1, PCH), F32),
+            pltpu.VMEM((1, PCH), F32),
             pltpu.VMEM((2 * DP, 1, RUN), F32),
             pltpu.VMEM((2 * DP, 1, RUN), F32),
             pltpu.VMEM((1, RUN), F32),
@@ -391,9 +389,8 @@
     cent, logt, mass = pl.pallas_call(
         hand_on,
         out_shape=tuple(jax.ShapeDtypeStruct(v.shape, v.dtype) for v in (cent, logt, mass)),
-        in_specs=[hbm, hbm, hbm],
-        out_specs=(hbm, hbm, hbm),
-        scratch_shapes=[dma((3,))],
+        in_specs=[vmem, vmem, vmem],
+        out_specs=(vmem, vmem, vmem),
         name="finish",
     )(cent, logt, mass)
     return cent, logt.reshape(RUN), mass.reshape(PART)

time: 74.6 us -> 62.7 us (0.84)
  Pallas kernels: 73.8 us -> 61.9 us
    pallas_call x1, Pallas kernels: 13.1 us -> 1.78 us  [per_device(): pl.pallas_call(hand_on, out_shape=tuple((jax.ShapeDtypeStruct(v.shape, v....]
where the time goes in v3:
time: 62.7 us; the launch traced here: 62.5 us
  Pallas kernels  61.9 us (99%)
  between operations  0.64 us (1%)
    pallas_call x1, Pallas kernels, per_device(): pl.pallas_call(kernel, out_shape=(jax.ShapeDtypeStruct((RUN, W), BF16), j...  60.1 us
    pallas_call x1, Pallas kernels, per_device(): pl.pallas_call(hand_on, out_shape=tuple((jax.ShapeDtypeStruct(v.shape, v....  1.78 us

profile of v3, /device:TPU:1, one launch (start us, length us, event | category | flops | bytes accessed | tf_op | source)
XLA Modules:
  0.0 62.5 jit_solution(12396203875693460804)
XLA Ops:
  0.6 60.1 %handover.1 = (bf16[128,1536]{1,0:T(8,128)(2,1)}, f32[1,128]{1,0:T(1,128)}, f32[1,64]{1,0:T(1,128)}) custom-call(s32[32,128]{1,0:T(8,128)} %bitcast.4, s32[1,128]{1,0:T(1,128)} %bitcast.5, bf16[4096,1536]{1,0:T(8,128)(2,1)} %e_hbm.1, bf16[512,1536]{1,0:T(8,128)(2,1)} %p_hbm.1), custom_call_target="tpu_custom_call" | custom-call | tf_op jit(solution)/shard_map/handover/pallas_call | solution.py:333
  60.8 1.8 %finish.1 = (bf16[128,1536]{1,0:T(8,128)(2,1)}, f32[1,128]{1,0:T(1,128)}, f32[1,64]{1,0:T(1,128)}) custom-call(bf16[128,1536]{1,0:T(8,128)(2,1)} %get-tuple-element.9.cent, f32[1,128]{1,0:T(1,128)} %get-tuple-element.10.logt, f32[1,64]{1,0:T(1,128)} %get-tuple-element.11.mass), custom_call_target="tpu_custom_call" | custom-call | tf_op jit(solution)/shard_map/finish/pallas_call | solution.py:389

commit v4 on v3

--- a/solution.py
+++ b/solution.py
@@ -14,7 +14,6 @@
 CAP = 48
 DP = 8
 SLOTS = DP * CAP
-EXT = W + RUN
 TILE = 256
 NTILE = W // TILE
 AHEAD = 2
@@ -27,15 +26,15 @@
 INV_SOFT = 1.0 / 0.5
 REWARD = 1.5
 
-RANGES = ((0, 256), (256, 512), (768, 896))
+RANGES = ((0, 256), (256, 512), (768, 768))
 SEND_AFTER = (0, 2, 5)
 
 
 def kernel(
     a_ref, label_ref, e_hbm, p_hbm,
-    cent_hbm, logt_hbm, mass_hbm,
-    e_v, oht, bt, slot_v, send, recv, par, cb, meta, scores, mch, sch, stat, fac, mp, sib_in, ms, mr, logt_v, mass_v,
-    e_sem, p_sem, row_ss, row_rs, par_ss, par_rs, cb_ss, cb_rs, meta_ss, meta_rs, stat_ss, stat_rs,
+    cent_hbm, logt_hbm, mr,
+    e_v, oht, place, slot_v, send, recv, id_send, id_recv, par, cb, meta, scores, mch, sch, stat, fac, mp, sib_in, ms, logt_v,
+    e_sem, p_sem, row_ss, row_rs, id_ss, id_rs, par_ss, par_rs, cb_ss, cb_rs, meta_ss, meta_rs, stat_ss, stat_rs,
     m1_ss, m1_rs, m2_ss, m2_rs, o_sem,
 ):
     d = lax.axis_index("dp")
@@ -97,12 +96,13 @@
     ahead = jnp.dot(earlier, jnp.ones((RUN, RUN), BF16), preferred_element_type=F32)
     base = ((lax.broadcasted_iota(jnp.int32, (256, RUN), 0) & 7) * CAP + 1).astype(F32)
     slot = jnp.sum((member * (within + ahead + base)).reshape(32, 8, RUN), axis=1) - 1.0
-    slot_v[0] = slot.astype(jnp.int32)
-    slot_v[1] = a & (RUN - 1)
-
-    for cp in e_copies[AHEAD : 2 * AHEAD]:
+    slot_v[...] = slot.astype(jnp.int32)
+    spot = ((a & (RUN - 1)) + 1).astype(F32)
+    for b in range(ROWS // RUN):
+        place[:, RUN * b : RUN * (b + 1)] = jnp.broadcast_to(spot[b : b + 1, :], (16, RUN)).astype(BF16)
+
+    for cp in e_copies[AHEAD:]:
         cp.start()
-    pl.semaphore_wait(barrier, len(partners))
 
     to_up = rcopy(p_hbm.at[pl.ds(0, HALF)], par.at[pl.ds(SLAB, HALF)], par_ss.at[0], par_rs.at[0], up)
     to_down = rcopy(p_hbm.at[pl.ds(HALF, HALF)], par.at[pl.ds(SLAB + HALF, HALF)], par_ss.at[1], par_rs.at[1], down)
@@ -117,18 +117,10 @@
         )
         for i in range(2)
     ]
-    to_up.start()
-    to_down.start()
-
-    for cp in e_copies[2 * AHEAD :]:
-        cp.start()
-
     def build(b, carry):
         cols = pl.ds(pl.multiple_of(b * RUN, RUN), RUN)
-        line = slot_v[0, pl.ds(b, 1), :]
-        place = slot_v[1, pl.ds(b, 1), :]
+        line = slot_v[pl.ds(b, 1), :]
         oht[:, cols] = (lax.broadcasted_iota(jnp.int32, (SLOTS, RUN), 0) == line).astype(F32).astype(BF16)
-        bt[:, cols] = (lax.broadcasted_iota(jnp.int32, (RUN, RUN), 0) == place).astype(F32).astype(BF16)
         return carry
 
     lax.fori_loop(0, ROWS // RUN, build, 0)
@@ -138,39 +130,59 @@
         return rcopy(
             send.at[dev[0], :, pl.ds(start, size)],
             recv.at[owner, :, pl.ds(start, size)],
-            row_ss.at[r - 1, g],
-            row_rs.at[r - 1, g],
+            row_ss.at[g],
+            row_rs.at[g],
             dev,
         )
 
+    def row_total(g):
+        start, size = RANGES[g]
+        cols = pl.ds(start, size)
+        part = pl.ds(0, DP - 1)
+        return rcopy(send.at[part, :, cols], recv.at[part, :, cols], row_ss.at[g], row_rs.at[g], row_peer(1))
+
+    id_total = rcopy(id_send.at[pl.ds(0, DP - 1)], id_recv.at[pl.ds(0, DP - 1)], id_ss, id_rs, row_peer(1))
+
     for n in range(NTILE):
         e_copies[n].wait()
+        part = jnp.dot(oht[...], e_v[n], preferred_element_type=F32)
+        send[:, :, TILE * n : TILE * (n + 1)] = part.astype(BF16).reshape(DP, CAP, TILE)
+        if n == 0:
+            pl.semaphore_wait(barrier, len(partners))
+        if n in SEND_AFTER:
+            for r in range(1, DP):
+                row_copy(r, SEND_AFTER.index(n), row_peer(r), d).start()
+        if n == 0:
+            to_up.start()
+            to_down.start()
         if n == 2:
             own_par.start()
             to_sib.start()
-        part = jnp.dot(oht[...], e_v[n], preferred_element_type=F32)
-        send[:, :, TILE * n : TILE * (n + 1)] = part.astype(BF16).reshape(DP, CAP, TILE)
-        if n == NTILE - 1:
-            ext = lax.dot_general(oht[...], bt[...], (((1,), (1,)), ((), ())), preferred_element_type=F32)
-            send[:, :, W:] = ext.astype(BF16).reshape(DP, CAP, RUN)
-        if n in SEND_AFTER:
+            spots = lax.dot_general(place[...], oht[...], (((1,), (1,)), ((), ())), preferred_element_type=F32)[:8]
+            lane = lax.broadcasted_iota(jnp.int32, (DP, SLOTS), 1)
+            mine = jnp.where(lane // CAP == lax.broadcasted_iota(jnp.int32, (DP, SLOTS), 0), spots, 0.0).astype(BF16)
+            lo = lax.broadcasted_iota(jnp.int32, (SLOTS, SLOTS), 0)
+            hi = lax.broadcasted_iota(jnp.int32, (SLOTS, SLOTS), 1)
+            shift = ((lo % CAP == hi % CAP) & (hi // CAP == d)).astype(F32).astype(BF16)
+            moved = jnp.dot(mine, shift, preferred_element_type=F32)
+            for i in range(DP):
+                id_send[i] = moved[i : i + 1, :]
             for r in range(1, DP):
-                row_copy(r, SEND_AFTER.index(n), row_peer(r), d).start()
+                dev = row_peer(r)
+                rcopy(id_send.at[dev[0]], id_recv.at[d], id_ss, id_rs, dev).start()
     recv[d] = send[d]
-
+    id_recv[d] = id_send[d]
     ms[...] = jnp.zeros_like(ms)
 
+    id_total.wait_recv()
+    ids = jnp.sum(id_recv[...], axis=0).astype(jnp.int32) - 1
+    onehot = (lax.broadcasted_iota(jnp.int32, (RUN, SLOTS), 0) == ids).astype(F32)
+    counts_col = jnp.sum(onehot, axis=1, keepdims=True)
+    onehot = onehot.astype(BF16)
+    counts_row = lax.dot_general(jnp.ones((16, SLOTS), BF16), onehot, (((1,), (1,)), ((), ())), preferred_element_type=F32)[:1]
     for g in range(len(RANGES)):
-        for r in range(1, DP):
-            row_copy(r, g, row_peer(r), (d + DP - r) % DP).wait_recv()
-
-    got = recv[...].reshape(SLOTS, EXT)
-    onehot = got[:, W:]
-    sums = lax.dot_general(onehot, got[:, :W], (((0,), (0,)), ((), ())), preferred_element_type=F32)
-    counts_col = lax.dot_general(
-        onehot, jnp.ones((SLOTS, RUN), BF16), (((0,), (0,)), ((), ())), preferred_element_type=F32
-    )[:, :1]
-    counts_row = jnp.sum(onehot.astype(F32), axis=0, keepdims=True)
+        row_total(g).wait_recv()
+    sums = jnp.dot(onehot, recv[...].reshape(SLOTS, W), preferred_element_type=F32)
     mean = sums / jnp.maximum(counts_col, 1.0)
     scale = jnp.sqrt(jnp.sum(mean * mean, axis=1, keepdims=True) + 1e-06)
     normed = (mean / scale).astype(BF16)
@@ -199,9 +211,9 @@
     z_second.start()
     y_second.start()
 
-    for r in range(1, DP):
-        for g in range(len(RANGES)):
-            row_copy(r, g, row_peer(r), d).wait_send()
+    for g in range(len(RANGES)):
+        row_total(g).wait_send()
+    id_total.wait_send()
     to_up.wait_recv()
     fwd_sib[0].start()
     to_down.wait_recv()
@@ -295,57 +307,54 @@
     for i in range(2 * DP):
         ms[i, :, :PART] = both[:, PART * i : PART * (i + 1)]
 
-    m2 = []
-    for r in range(1, DP):
-        m2.append(rcopy(ms.at[(d + r) % DP], mr.at[d], m2_ss.at[r - 1], m2_rs.at[d], row_peer(r)))
+    def mass_copy(line, to_line, dev):
+        rcopy(ms.at[line], mr.at[to_line], m2_ss, m2_rs, dev).start()
+
     for r in range(4):
         lo, hi = (d + r) % 4, 4 + (d + r) % 4
-        m2.append(rcopy(ms.at[DP + lo], mr.at[DP + d], m2_ss.at[7 + r], m2_rs.at[DP + d], (lo, cent_of(zhi, ym, k))))
-        m2.append(rcopy(ms.at[DP + hi], mr.at[DP + d], m2_ss.at[11 + r], m2_rs.at[DP + d], (hi, cent_of(zhi, yp, k))))
-    for cp in m2:
-        cp.start()
-    mr[d] = ms[d]
+        mass_copy(DP + lo, DP + d, (lo, cent_of(zhi, ym, k)))
+        mass_copy(DP + hi, DP + d, (hi, cent_of(zhi, yp, k)))
     for r in range(1, DP):
-        src = (d + r) % DP
-        rcopy(ms.at[0], mr.at[src], m2_ss.at[0], m2_rs.at[src], row_peer(r)).wait_recv()
-    for r in range(DP):
-        rcopy(ms.at[0], mr.at[DP + r], m2_ss.at[0], m2_rs.at[DP + r], row_peer(1)).wait_recv()
-    mass_v[...] = jnp.sum(mr[...], axis=0)[:, :PART]
-    mass_out = pltpu.make_async_copy(mass_v, mass_hbm, o_sem.at[2])
-    mass_out.start()
-
-    for cp in [to_sib_mass, *stats.values(), *m2]:
+        mass_copy((d + r) % DP, d, row_peer(r))
+    own_mass = pltpu.make_async_copy(ms.at[d], mr.at[d], o_sem.at[2])
+    own_mass.start()
+    for cp in [to_sib_mass, *stats.values()]:
         cp.wait_send()
     logt_out.wait()
-    mass_out.wait()
-
-
-def hand_on(cent, logt, mass, cent_out, logt_out, mass_out):
+    own_mass.wait()
+    lines = pl.ds(0, 2 * DP - 1)
+    rcopy(ms.at[lines], mr.at[lines], m2_ss, m2_rs, row_peer(1)).wait()
+
+
+def hand_on(cent, logt, terms, cent_out, logt_out, mass_out):
     cent_out[...] = cent[...]
     logt_out[...] = logt[...]
-    mass_out[...] = mass[...]
+    mass_out[...] = jnp.sum(terms[...], axis=0)[:, :PART]
 
 
 def per_device(embeddings, assignments, parents, starting_coarse_label):
     vmem = pl.BlockSpec(memory_space=pltpu.VMEM)
     hbm = pl.BlockSpec(memory_space=pltpu.HBM)
+    anywhere = pl.BlockSpec(memory_space=pl.ANY)
     dma = pltpu.SemaphoreType.DMA
-    cent, logt, mass = pl.pallas_call(
+    cent, logt, terms = pl.pallas_call(
         kernel,
         out_shape=(
             jax.ShapeDtypeStruct((RUN, W), BF16),
             jax.ShapeDtypeStruct((1, RUN), F32),
-            jax.ShapeDtypeStruct((1, PART), F32),
+            jax.ShapeDtypeStruct((2 * DP, 1, RUN), F32),
         ),
         in_specs=[vmem, vmem, hbm, hbm],
-        out_specs=(hbm, hbm, hbm),
+        out_specs=(anywhere, anywhere, anywhere),
         scratch_shapes=[
             pltpu.VMEM((NTILE, ROWS, TILE), BF16),
             pltpu.VMEM((SLOTS, ROWS), BF16),
-            pltpu.VMEM((RUN, ROWS), BF16),
-            pltpu.VMEM((2, 32, RUN), jnp.int32),
-            pltpu.VMEM((DP, CAP, EXT), BF16),
-            pltpu.VMEM((DP, CAP, EXT), BF16),
+            pltpu.VMEM((16, ROWS), BF16),
+            pltpu.VMEM((32, RUN), jnp.int32),
+            pltpu.VMEM((DP, CAP, W), BF16),
+            pltpu.VMEM((DP, CAP, W), BF16),
+            pltpu.VMEM((DP, 1, SLOTS), F32),
+            pltpu.VMEM((DP, 1, SLOTS), F32),
             pltpu.VMEM((NPCH * PCH, W), BF16),
             pltpu.VMEM((4, RUN, W), BF16),
             pltpu.VMEM((4, 8, RUN), F32),
@@ -357,13 +366,13 @@
             pltpu.VMEM((NPCH, 1, PCH), F32),
             pltpu.VMEM((1, PCH), F32),
             pltpu.VMEM((2 * DP, 1, RUN), F32),
-            pltpu.VMEM((2 * DP, 1, RUN), F32),
             pltpu.VMEM((1, RUN), F32),
-            pltpu.VMEM((1, PART), F32),
             dma((NTILE,)),
             dma,
-            dma((DP - 1, len(RANGES))),
-            dma((DP - 1, len(RANGES))),
+            dma((len(RANGES),)),
+            dma((len(RANGES),)),
+            dma,
+            dma,
             dma((5,)),
             dma((5,)),
             dma((6,)),
@@ -374,11 +383,11 @@
             dma((3,)),
             dma,
             dma,
-            dma((2 * DP - 1,)),
-            dma((2 * DP,)),
+            dma,
+            dma,
             dma((3,)),
         ],
-        compiler_params=pltpu.CompilerParams(collective_id=0, has_side_effects=True, vmem_limit_bytes=56 << 20),
+        compiler_params=pltpu.CompilerParams(collective_id=0, has_side_effects=True, vmem_limit_bytes=53 << 20),
         name="handover",
     )(
         assignments.reshape(32, RUN),
@@ -388,11 +397,16 @@
     )
     cent, logt, mass = pl.pallas_call(
         hand_on,
-        out_shape=tuple(jax.ShapeDtypeStruct(v.shape, v.dtype) for v in (cent, logt, mass)),
+        out_shape=(
+            jax.ShapeDtypeStruct((RUN, W), BF16),
+            jax.ShapeDtypeStruct((1, RUN), F32),
+            jax.ShapeDtypeStruct((1, PART), F32),
+        ),
         in_specs=[vmem, vmem, vmem],
         out_specs=(vmem, vmem, vmem),
+        compiler_params=pltpu.CompilerParams(vmem_limit_bytes=2 << 20),
         name="finish",
-    )(cent, logt, mass)
+    )(cent, logt, terms)
     return cent, logt.reshape(RUN), mass.reshape(PART)
 
 

time: 62.7 us -> 59.4 us (0.947)
  Pallas kernels: 61.9 us -> 57.2 us
  local copies, waits for them, and re-layouts: 0 us -> 1.37 us
    pallas_call x1, Pallas kernels: 60.1 us -> 56.4 us  [per_device(): pl.pallas_call(kernel, out_shape=(jax.ShapeDtypeStruct((RUN, W), BF16), j...]
    unnamed x0 -> x4, local copies, waits for them, and re-layouts: none -> 1.37 us
    pallas_call x1, Pallas kernels: 1.78 us -> 0.78 us  [per_device(): pl.pallas_call(hand_on, out_shape=(jax.ShapeDtypeStruct((RUN, W), BF16),...]
where the time goes in v4:
time: 59.4 us; the launch traced here: 59.2 us
  Pallas kernels  57.2 us (96%)
  local copies, waits for them, and re-layouts  1.37 us (2%)
  between operations  0.65 us (1%)
    pallas_call x1, Pallas kernels, per_device(): pl.pallas_call(kernel, out_shape=(jax.ShapeDtypeStruct((RUN, W), BF16), j...  56.4 us
    unnamed x4, local copies, waits for them, and re-layouts  1.37 us

profile of v4, /device:TPU:1, one launch (start us, length us, event | category | flops | bytes accessed | tf_op | source)
XLA Modules:
  0.0 59.2 jit_solution(15922613377950413851)
XLA Ops:
  0.6 0.0 copy-start
  0.6 0.7 %copy-done = s32[4096]{0:T(1024)S(1)} copy-done((s32[4096]{0:T(1024)S(1)}, s32[4096]{0:T(1024)}, u32[]{:S(2)}) %copy-start) | copy-done | bytes 16408
  1.3 0.0 copy-start.1
  1.4 0.7 %copy-done.1 = s32[128]{0:T(128)S(1)} copy-done((s32[128]{0:T(128)S(1)}, s32[128]{0:T(128)}, u32[]{:S(2)}) %copy-start.1) | copy-done | bytes 536
  2.0 56.4 %handover.1 = (bf16[128,1536]{1,0:T(8,128)(2,1)S(1)}, f32[1,128]{1,0:T(1,128)S(1)}, f32[16,1,128]{2,1,0:T(1,128)S(1)}) custom-call(s32[32,128]{1,0:T(8,128)S(1)} %bitcast.4, s32[1,128]{1,0:T(1,128)S(1)} %bitcast.5, bf16[4096,1536]{1,0:T(8,128)(2,1)} %e_hbm.1, bf16[512,1536]{1,0:T(8,128)(2,1)} %p_hbm.1), custom_call_target="tpu_custom_call" | custom-call | tf_op jit(solution)/shard_map/handover/pallas_call | solution.py:340
  58.4 0.8 %finish.1 = (bf16[128,1536]{1,0:T(8,128)(2,1)}, f32[1,128]{1,0:T(1,128)}, f32[1,64]{1,0:T(1,128)}) custom-call(bf16[128,1536]{1,0:T(8,128)(2,1)S(1)} %get-tuple-element.9.cent, f32[1,128]{1,0:T(1,128)S(1)} %get-tuple-element.10.logt, f32[16,1,128]{2,1,0:T(1,128)S(1)} %get-tuple-element.11.terms), custom_call_target="tpu_custom_call" | custom-call | tf_op jit(solution)/shard_map/finish/pallas_call | solution.py:398
Async XLA Ops:
  0.6 0.7 %copy-start = (s32[4096]{0:T(1024)S(1)}, s32[4096]{0:T(1024)}, u32[]{:S(2)}) copy-start(s32[4096]{0:T(1024)} %param.5) | copy-start | bytes 49156
  1.3 0.7 %copy-start.1 = (s32[128]{0:T(128)S(1)}, s32[128]{0:T(128)}, u32[]{:S(2)}) copy-start(s32[128]{0:T(128)} %param.7) | copy-start | bytes 1540

commit v5 on v4

--- a/solution.py
+++ b/solution.py
@@ -16,7 +16,6 @@
 SLOTS = DP * CAP
 TILE = 256
 NTILE = W // TILE
-AHEAD = 2
 ROWS = 4096
 SLAB = 512
 PART = 64
@@ -31,11 +30,11 @@
 
 
 def kernel(
-    a_ref, label_ref, e_hbm, p_hbm,
+    a_hbm, label_hbm, e_hbm, p_hbm,
     cent_hbm, logt_hbm, mr,
-    e_v, oht, place, slot_v, send, recv, id_send, id_recv, par, cb, meta, scores, mch, sch, stat, fac, mp, sib_in, ms, logt_v,
+    a_v, label_v, e_v, oht, place, slot_v, send, recv, id_send, id_recv, par, cb, meta, scores, mch, sch, stat, fac, mp, sib_in, ms, logt_v,
     e_sem, p_sem, row_ss, row_rs, id_ss, id_rs, par_ss, par_rs, cb_ss, cb_rs, meta_ss, meta_rs, stat_ss, stat_rs,
-    m1_ss, m1_rs, m2_ss, m2_rs, o_sem,
+    m1_ss, m1_rs, m2_ss, m2_rs, o_sem, in_sem,
 ):
     d = lax.axis_index("dp")
     c = lax.axis_index("cent")
@@ -66,6 +65,15 @@
             src_ref=src, dst_ref=dst, send_sem=ss, recv_sem=rs, device_id=dev, device_id_type=MESH
         )
 
+    load_a = pltpu.make_async_copy(a_hbm, a_v, in_sem.at[0])
+    load_label = pltpu.make_async_copy(label_hbm, label_v, in_sem.at[1])
+    e_copies = [
+        pltpu.make_async_copy(e_hbm.at[:, pl.ds(TILE * n, TILE)], e_v.at[n], e_sem.at[n]) for n in range(NTILE)
+    ]
+    own_par = pltpu.make_async_copy(p_hbm, par.at[pl.ds(0, SLAB)], p_sem)
+    load_a.start()
+    e_copies[0].start()
+
     barrier = pltpu.get_barrier_semaphore()
     mass_from = cent_of(zhi, jnp.where(d < 4, yp, ym), k)
     partners = [row_peer(r) for r in range(1, DP)] + [group[1], group[2], group[3], sibling, up, down]
@@ -73,14 +81,11 @@
     for dev in partners:
         pl.semaphore_signal(barrier, inc=1, device_id=dev, device_id_type=MESH)
 
-    e_copies = [
-        pltpu.make_async_copy(e_hbm.at[:, pl.ds(TILE * n, TILE)], e_v.at[n], e_sem.at[n]) for n in range(NTILE)
-    ]
-    for cp in e_copies[:AHEAD]:
-        cp.start()
-    own_par = pltpu.make_async_copy(p_hbm, par.at[pl.ds(0, SLAB)], p_sem)
-
-    a = a_ref[...]
+    e_copies[1].start()
+    load_label.start()
+    load_a.wait()
+
+    a = a_v[...]
     rel = lax.shift_right_logical(a, 7) - c * DP
     run_id = lax.broadcasted_iota(jnp.int32, (32, 8, RUN), 1)
     member = (rel[:, None, :] == run_id).astype(F32).reshape(256, RUN)
@@ -101,9 +106,6 @@
     for b in range(ROWS // RUN):
         place[:, RUN * b : RUN * (b + 1)] = jnp.broadcast_to(spot[b : b + 1, :], (16, RUN)).astype(BF16)
 
-    for cp in e_copies[AHEAD:]:
-        cp.start()
-
     to_up = rcopy(p_hbm.at[pl.ds(0, HALF)], par.at[pl.ds(SLAB, HALF)], par_ss.at[0], par_rs.at[0], up)
     to_down = rcopy(p_hbm.at[pl.ds(HALF, HALF)], par.at[pl.ds(SLAB + HALF, HALF)], par_ss.at[1], par_rs.at[1], down)
     to_sib = rcopy(p_hbm, par.at[pl.ds(2 * SLAB, SLAB)], par_ss.at[2], par_rs.at[2], sibling)
@@ -124,6 +126,9 @@
         return carry
 
     lax.fori_loop(0, ROWS // RUN, build, 0)
+
+    for cp in e_copies[2:]:
+        cp.start()
 
     def row_copy(r, g, dev, owner):
         start, size = RANGES[g]
@@ -189,8 +194,9 @@
     cb[0] = normed
     cent_out = pltpu.make_async_copy(cb.at[0], cent_hbm, o_sem.at[0])
     cent_out.start()
+    load_label.wait()
     meta[0, 0:1, :] = counts_row.astype(BF16).astype(F32)
-    meta[0, 1:2, :] = label_ref[...].astype(F32)
+    meta[0, 1:2, :] = label_v[...].astype(F32)
     meta[0, 2:8, :] = jnp.zeros((6, RUN), F32)
 
     def half(slot_from, slot_to, h, idx, dev):
@@ -206,7 +212,7 @@
     z_first.start()
     y_first.start()
     metas = {q: rcopy(meta.at[0], meta.at[q], meta_ss.at[q - 1], meta_rs.at[q - 1], group[q]) for q in (1, 2, 3)}
-    for q in (1, 2, 3):
+    for q in (3, 2, 1):
         metas[q].start()
     z_second.start()
     y_second.start()
@@ -271,7 +277,7 @@
         stat[0, j : j + 1, :] = m_loc[:, RUN * j : RUN * (j + 1)]
         stat[0, 4 + j : 5 + j, :] = s_loc[:, RUN * j : RUN * (j + 1)]
     stats = {q: rcopy(stat.at[0], stat.at[q], stat_ss.at[q - 1], stat_rs.at[q - 1], group[q]) for q in (1, 2, 3)}
-    for q in (1, 2, 3):
+    for q in (3, 2, 1):
         stats[q].start()
     for cp in [y_second, fwd_y, fwd_z]:
         cp.wait_send()
@@ -337,6 +343,7 @@
     hbm = pl.BlockSpec(memory_space=pltpu.HBM)
     anywhere = pl.BlockSpec(memory_space=pl.ANY)
     dma = pltpu.SemaphoreType.DMA
+    operands = (assignments.reshape(32, RUN), starting_coarse_label.reshape(1, RUN), embeddings, parents)
     cent, logt, terms = pl.pallas_call(
         kernel,
         out_shape=(
@@ -344,9 +351,11 @@
             jax.ShapeDtypeStruct((1, RUN), F32),
             jax.ShapeDtypeStruct((2 * DP, 1, RUN), F32),
         ),
-        in_specs=[vmem, vmem, hbm, hbm],
+        in_specs=[hbm, hbm, hbm, hbm],
         out_specs=(anywhere, anywhere, anywhere),
         scratch_shapes=[
+            pltpu.VMEM((32, RUN), jnp.int32),
+            pltpu.VMEM((1, RUN), jnp.int32),
             pltpu.VMEM((NTILE, ROWS, TILE), BF16),
             pltpu.VMEM((SLOTS, ROWS), BF16),
             pltpu.VMEM((16, ROWS), BF16),
@@ -386,14 +395,12 @@
             dma,
             dma,
             dma((3,)),
+            dma((2,)),
         ],
-        compiler_params=pltpu.CompilerParams(collective_id=0, has_side_effects=True, vmem_limit_bytes=53 << 20),
+        compiler_params=pltpu.CompilerParams(collective_id=0, has_side_effects=True, vmem_limit_bytes=52 << 20),
         name="handover",
     )(
-        assignments.reshape(32, RUN),
-        starting_coarse_label.reshape(1, RUN),
-        embeddings,
-        parents,
+        *(pltpu.with_memory_space_constraint(v, pltpu.HBM) for v in operands),
     )
     cent, logt, mass = pl.pallas_call(
         hand_on,

time: 59.4 us -> 58.2 us (0.980)
  local copies, waits for them, and re-layouts: 1.37 us -> 0 us
    unnamed x4 -> x0, local copies, waits for them, and re-layouts: 1.37 us -> none
where the time goes in v5:
time: 58.2 us; the launch traced here: 58.1 us
  Pallas kernels  57.4 us (99%)
  between operations  0.64 us (1%)
    pallas_call x1, Pallas kernels, per_device(): pl.pallas_call(kernel, out_shape=(jax.ShapeDtypeStruct((RUN, W), BF16), j...  56.6 us

profile of v5, /device:TPU:1, one launch (start us, length us, event | category | flops | bytes accessed | tf_op | source)
XLA Modules:
  0.0 58.1 jit_solution(4176776334870983448)
XLA Ops:
  0.6 56.6 %handover.1 = (bf16[128,1536]{1,0:T(8,128)(2,1)S(1)}, f32[1,128]{1,0:T(1,128)S(1)}, f32[16,1,128]{2,1,0:T(1,128)S(1)}) custom-call(s32[32,128]{1,0:T(8,128)} %bitcast.4, s32[1,128]{1,0:T(1,128)} %bitcast.5, bf16[4096,1536]{1,0:T(8,128)(2,1)} %e_hbm.1, bf16[512,1536]{1,0:T(8,128)(2,1)} %p_hbm.1), custom_call_target="tpu_custom_call" | custom-call | tf_op jit(solution)/shard_map/handover/pallas_call | solution.py:347
  57.3 0.8 %finish.1 = (bf16[128,1536]{1,0:T(8,128)(2,1)}, f32[1,128]{1,0:T(1,128)}, f32[1,64]{1,0:T(1,128)}) custom-call(bf16[128,1536]{1,0:T(8,128)(2,1)S(1)} %get-tuple-element.9.cent, f32[1,128]{1,0:T(1,128)S(1)} %get-tuple-element.10.logt, f32[16,1,128]{2,1,0:T(1,128)S(1)} %get-tuple-element.11.terms), custom_call_target="tpu_custom_call" | custom-call | tf_op jit(solution)/shard_map/finish/pallas_call | solution.py:405

commit v6 on v5

--- a/solution.py
+++ b/solution.py
@@ -19,9 +19,9 @@
 ROWS = 4096
 SLAB = 512
 PART = 64
-PCH = 1024
-NPCH = 2
-HALF = 256
+EARLY, LATE = 1536, 512
+BLK = 128
+PIECES = (0, 2, 1, 3)
 INV_SOFT = 1.0 / 0.5
 REWARD = 1.5
 
@@ -32,7 +32,7 @@
 def kernel(
     a_hbm, label_hbm, e_hbm, p_hbm,
     cent_hbm, logt_hbm, mr,
-    a_v, label_v, e_v, oht, place, slot_v, send, recv, id_send, id_recv, par, cb, meta, scores, mch, sch, stat, fac, mp, sib_in, ms, logt_v,
+    a_v, label_v, e_v, oht, place, slot_v, send, recv, id_send, id_recv, par, cb, meta, scores_e, scores_l, mch, sch, stat, fac, mp, sib_in, ms, logt_v,
     e_sem, p_sem, row_ss, row_rs, id_ss, id_rs, par_ss, par_rs, cb_ss, cb_rs, meta_ss, meta_rs, stat_ss, stat_rs,
     m1_ss, m1_rs, m2_ss, m2_rs, o_sem, in_sem,
 ):
@@ -47,15 +47,29 @@
         return zh * 8 + yy * 2 + kk
 
     yp, ym, y2 = (y + 1) % 4, (y + 3) % 4, (y + 2) % 4
-    flip_d = d - zlo + (1 - zlo)
+    x = d // 2
+    q = x % 2
+    xp, xm = (x + 1) % 4, (x + 3) % 4
+    other_z = cent_of(1 - zhi, y, k)
+    ZN, XM, XP, ZXM, ZXP = 1, 2, 3, 4, 5
     group = {
-        1: (flip_d, cent_of(1 - zhi, y, k)),
-        2: (d, cent_of(zhi, y2, k)),
-        3: (flip_d, cent_of(1 - zhi, y2, k)),
+        ZN: (x * 2 + 1 - zlo, other_z),
+        XM: (xm * 2 + zlo, c),
+        XP: (xp * 2 + zlo, c),
+        ZXM: (xm * 2 + 1 - zlo, other_z),
+        ZXP: (xp * 2 + 1 - zlo, other_z),
     }
+    inverse = {ZN: ZN, XM: XP, XP: XM, ZXM: ZXP, ZXP: ZXM}
     sibling = (d, cent_of(zhi, y, 1 - k))
     up = (d, cent_of(zhi, yp, k))
     down = (d, cent_of(zhi, ym, k))
+    y_of = (y, ym, yp, y2)
+
+    def owner(t, ra, rb):
+        a, b = (x // 2 + ra) % 2, (zlo + rb) % 2
+        return 4 * t + 2 * a + b, ((2 * a + q) * 2 + b, cent_of(zhi, y_of[t], k))
+
+    owners = [(t, ra, rb) for t in (3, 2, 1, 0) for ra in (1, 0) for rb in (1, 0) if (t, ra, rb) != (0, 0, 0)]
 
     def row_peer(r):
         return ((d + r) % DP, c)
@@ -70,14 +84,20 @@
     e_copies = [
         pltpu.make_async_copy(e_hbm.at[:, pl.ds(TILE * n, TILE)], e_v.at[n], e_sem.at[n]) for n in range(NTILE)
     ]
-    own_par = pltpu.make_async_copy(p_hbm, par.at[pl.ds(0, SLAB)], p_sem)
+    def mine(a):
+        return p_hbm.at[pl.ds(pl.multiple_of(2 * BLK * a + BLK * q, BLK), BLK)]
+
+    def place_of(core, t, a=0, n=1):
+        start = (EARLY + 256 * core if t == 3 else 768 * core + 256 * t) + BLK * a
+        return par.at[pl.ds(start, BLK * n)]
+
+    own_par = [pltpu.make_async_copy(mine(a), place_of(0, 0, a), p_sem.at[a]) for a in range(2)]
     load_a.start()
     e_copies[0].start()
 
     barrier = pltpu.get_barrier_semaphore()
-    mass_from = cent_of(zhi, jnp.where(d < 4, yp, ym), k)
-    partners = [row_peer(r) for r in range(1, DP)] + [group[1], group[2], group[3], sibling, up, down]
-    partners += [((d + r) % DP, mass_from) for r in range(DP)]
+    partners = [row_peer(r) for r in range(1, DP)] + [group[ZN], group[ZXM], group[ZXP], sibling]
+    partners += [owner(*o)[1] for o in owners if o[0] != 0]
     for dev in partners:
         pl.semaphore_signal(barrier, inc=1, device_id=dev, device_id_type=MESH)
 
@@ -106,19 +126,17 @@
     for b in range(ROWS // RUN):
         place[:, RUN * b : RUN * (b + 1)] = jnp.broadcast_to(spot[b : b + 1, :], (16, RUN)).astype(BF16)
 
-    to_up = rcopy(p_hbm.at[pl.ds(0, HALF)], par.at[pl.ds(SLAB, HALF)], par_ss.at[0], par_rs.at[0], up)
-    to_down = rcopy(p_hbm.at[pl.ds(HALF, HALF)], par.at[pl.ds(SLAB + HALF, HALF)], par_ss.at[1], par_rs.at[1], down)
-    to_sib = rcopy(p_hbm, par.at[pl.ds(2 * SLAB, SLAB)], par_ss.at[2], par_rs.at[2], sibling)
-    fwd_sib = [
-        rcopy(
-            par.at[pl.ds(SLAB + i * HALF, HALF)],
-            par.at[pl.ds(3 * SLAB + i * HALF, HALF)],
-            par_ss.at[3 + i],
-            par_rs.at[3 + i],
-            sibling,
-        )
-        for i in range(2)
-    ]
+    def par_copy(src, dst, idx, dev):
+        return rcopy(src, dst, par_ss.at[idx], par_rs.at[idx], dev)
+
+    to_up = [par_copy(mine(a), place_of(0, 1, a), a, up) for a in range(2)]
+    to_down = [par_copy(mine(a), place_of(0, 2, a), 2 + a, down) for a in range(2)]
+    on_up = par_copy(place_of(0, 1, 0), place_of(0, 3, 0), 4, up)
+    on_down = par_copy(place_of(0, 2, 1), place_of(0, 3, 1), 5, down)
+    to_sib = [par_copy(mine(a), place_of(1, 0, a), 6 + a, sibling) for a in range(2)]
+    sib_early = [par_copy(place_of(0, t, 0, 2), place_of(1, t, 0, 2), 7 + t, sibling) for t in (1, 2)]
+    sib_late = [par_copy(place_of(0, 3, a), place_of(1, 3, a), 10 + a, sibling) for a in range(2)]
+
     def build(b, carry):
         cols = pl.ds(pl.multiple_of(b * RUN, RUN), RUN)
         line = slot_v[pl.ds(b, 1), :]
@@ -158,11 +176,11 @@
             for r in range(1, DP):
                 row_copy(r, SEND_AFTER.index(n), row_peer(r), d).start()
         if n == 0:
-            to_up.start()
-            to_down.start()
+            for cp in (to_up[0], to_down[1], to_up[1], to_down[0]):
+                cp.start()
         if n == 2:
-            own_par.start()
-            to_sib.start()
+            for cp in (*own_par, *to_sib):
+                cp.start()
             spots = lax.dot_general(place[...], oht[...], (((1,), (1,)), ((), ())), preferred_element_type=F32)[:8]
             lane = lax.broadcasted_iota(jnp.int32, (DP, SLOTS), 1)
             mine = jnp.where(lane // CAP == lax.broadcasted_iota(jnp.int32, (DP, SLOTS), 0), spots, 0.0).astype(BF16)
@@ -199,112 +217,153 @@
     meta[0, 1:2, :] = label_v[...].astype(F32)
     meta[0, 2:8, :] = jnp.zeros((6, RUN), F32)
 
-    def half(slot_from, slot_to, h, idx, dev):
-        rows = pl.ds(64 * h, 64)
-        return rcopy(cb.at[slot_from, rows], cb.at[slot_to, rows], cb_ss.at[idx], cb_rs.at[idx], dev)
-
-    z_first = half(0, 1, 0, 0, group[1])
-    z_second = half(0, 1, 1, 1, group[1])
-    y_first = half(0, 2, 1, 2, group[2])
-    y_second = half(0, 2, 0, 3, group[2])
-    fwd_y = half(1, 3, 0, 4, group[2])
-    fwd_z = half(2, 3, 1, 5, group[1])
-    z_first.start()
-    y_first.start()
-    metas = {q: rcopy(meta.at[0], meta.at[q], meta_ss.at[q - 1], meta_rs.at[q - 1], group[q]) for q in (1, 2, 3)}
-    for q in (3, 2, 1):
-        metas[q].start()
-    z_second.start()
-    y_second.start()
-
+    def cent_copy(src, dst, start, size, idx, dev):
+        rows = pl.ds(start, size)
+        return rcopy(cb.at[src, rows], cb.at[dst, rows], cb_ss.at[idx], cb_rs.at[idx], dev)
+
+    over_z = [cent_copy(0, 2, 32 * i, 32, i, group[ZN]) for i in range(4)]
+    over_x = [cent_copy(0, 1, 64 * h, 64, 4 + h, group[(XP, XM)[h]]) for h in range(2)]
+    pass_on = [cent_copy(2, 3, 32 * i, 32, 6 + i, group[(XP, XM)[i // 2]]) for i in range(4)]
+    over_z[PIECES[0]].start()
+    for cp in over_x:
+        cp.start()
+    for i in PIECES[1:]:
+        over_z[i].start()
+    metas = {p: rcopy(meta.at[0], meta.at[inverse[p]], meta_ss.at[p], meta_rs.at[inverse[p]], group[p]) for p in group}
+    for p in (ZXM, ZXP, ZN, XM, XP):
+        metas[p].start()
+
+    def arrived(p):
+        return rcopy(meta.at[0], meta.at[p], meta_ss.at[p], meta_rs.at[p], group[p])
+
+    to_up[0].wait_recv()
+    on_up.start()
+    to_down[1].wait_recv()
+    on_down.start()
     for g in range(len(RANGES)):
         row_total(g).wait_send()
     id_total.wait_send()
-    to_up.wait_recv()
-    fwd_sib[0].start()
-    to_down.wait_recv()
-    fwd_sib[1].start()
-    z_first.wait_recv()
-    fwd_y.start()
-    y_first.wait_recv()
-    fwd_z.start()
-
-    own_par.wait()
-    to_sib.wait_recv()
-    for cp in fwd_sib:
+    to_up[1].wait_recv()
+    sib_early[0].start()
+    to_down[0].wait_recv()
+    sib_early[1].start()
+    for i in PIECES[:2]:
+        over_z[i].wait_recv()
+        pass_on[i].start()
+    for cp in own_par:
+        cp.wait()
+    for cp in (*to_sib, *over_x, *sib_early):
         cp.wait_recv()
-    for q in (1, 2, 3):
-        metas[q].wait_recv()
-
-    def parent_ids(i):
-        core = jnp.where(i == 0, k, 1 - k)
-        mine, low, high = (cent_of(zhi, v, core) * SLAB for v in (y, ym, yp))
-        line = lax.broadcasted_iota(jnp.int32, (PCH, 2 * RUN), 0)
-        return (line & (SLAB - 1)) + jnp.where(line < SLAB, mine, jnp.where(line < SLAB + HALF, low, high))
-
-    def score(pair):
-        cols = pl.ds(2 * RUN * pair, 2 * RUN)
+    for p in group:
+        arrived(p).wait_recv()
+
+    low_lanes = lax.broadcasted_iota(jnp.int32, (1, RUN), 1) < RUN // 2
+
+    def halves(low, high):
+        return jnp.where(low_lanes, low, high)
+
+    def meta_line(i):
+        return [
+            meta[0, i : i + 1, :],
+            halves(meta[XM, i : i + 1, :], meta[XP, i : i + 1, :]),
+            meta[ZN, i : i + 1, :],
+            halves(meta[ZXM, i : i + 1, :], meta[ZXP, i : i + 1, :]),
+        ]
+
+    weights, labels = meta_line(0), meta_line(1)
+
+    def first_ids(early):
+        found = []
+        for core in (k, 1 - k):
+            for t in (0, 1, 2) if early else (3,):
+                for a in range(2):
+                    found.append(cent_of(zhi, y_of[t], core) * SLAB + 2 * BLK * a + BLK * q)
+        return found
+
+    def score(pair, early):
+        cols = slice(2 * RUN * pair, 2 * RUN * (pair + 1))
         block = cb[2 * pair : 2 * pair + 2].reshape(2 * RUN, W)
-        label = jnp.concatenate([meta[2 * pair, 1:2, :], meta[2 * pair + 1, 1:2, :]], axis=1).astype(jnp.int32)
-
-        def step(i, carry):
-            s = lax.dot_general(
-                par[pl.ds(pl.multiple_of(i * PCH, PCH), PCH), :], block, (((1,), (1,)), ((), ())), preferred_element_type=F32
-            )
-            s = s * INV_SOFT + jnp.where(parent_ids(i) == label, REWARD, 0.0)
-            top = jnp.max(s, axis=0, keepdims=True)
-            e = jnp.exp(s - top)
-            scores[i, :, cols] = e
-            mch[pl.ds(i, 1), cols] = top
-            sch[pl.ds(i, 1), cols] = jnp.sum(e, axis=0, keepdims=True)
-            return carry
-
-        lax.fori_loop(0, NPCH, step, 0)
-
-    z_second.wait_recv()
-    score(0)
-    for cp in [to_up, to_down, to_sib, *fwd_sib, *metas.values(), z_first, z_second, y_first]:
+        label = jnp.concatenate([labels[2 * pair], labels[2 * pair + 1]], axis=1).astype(jnp.int32)
+        some = par[:EARLY, :] if early else par[EARLY:, :]
+        s = lax.dot_general(some, block, (((1,), (1,)), ((), ())), preferred_element_type=F32)
+        line = lax.broadcasted_iota(jnp.int32, (BLK, 2 * RUN), 0)
+        s = jnp.concatenate(
+            [
+                s[BLK * i : BLK * (i + 1)] * INV_SOFT + jnp.where(line == label - first, REWARD, 0.0)
+                for i, first in enumerate(first_ids(early))
+            ],
+            axis=0,
+        )
+        top = jnp.max(s, axis=0, keepdims=True)
+        e = jnp.exp(s - top)
+        (scores_e if early else scores_l)[:, cols] = e
+        row = 0 if early else 1
+        mch[row : row + 1, cols] = top
+        sch[row : row + 1, cols] = jnp.sum(e, axis=0, keepdims=True)
+
+    score(0, True)
+    for i in PIECES[2:]:
+        over_z[i].wait_recv()
+        pass_on[i].start()
+    on_up.wait_recv()
+    sib_late[0].start()
+    on_down.wait_recv()
+    sib_late[1].start()
+    for cp in (*to_up, *to_down, *to_sib, *sib_early, *metas.values(), *over_x):
         cp.wait_send()
     cent_out.wait()
-    y_second.wait_recv()
-    fwd_y.wait_recv()
-    fwd_z.wait_recv()
-    score(1)
+    for cp in sib_late:
+        cp.wait_recv()
+    score(0, False)
+    for cp in pass_on:
+        cp.wait_recv()
+    score(1, True)
+    score(1, False)
 
     m_loc = jnp.max(mch[...], axis=0, keepdims=True)
     s_loc = jnp.sum(sch[...] * jnp.exp(mch[...] - m_loc), axis=0, keepdims=True)
     for j in range(4):
         stat[0, j : j + 1, :] = m_loc[:, RUN * j : RUN * (j + 1)]
         stat[0, 4 + j : 5 + j, :] = s_loc[:, RUN * j : RUN * (j + 1)]
-    stats = {q: rcopy(stat.at[0], stat.at[q], stat_ss.at[q - 1], stat_rs.at[q - 1], group[q]) for q in (1, 2, 3)}
-    for q in (3, 2, 1):
-        stats[q].start()
-    for cp in [y_second, fwd_y, fwd_z]:
+    stats = {p: rcopy(stat.at[0], stat.at[inverse[p]], stat_ss.at[p], stat_rs.at[inverse[p]], group[p]) for p in group}
+    for p in (ZXM, ZXP, ZN, XM, XP):
+        stats[p].start()
+    for cp in (*over_z, *pass_on, on_up, on_down, *sib_late):
         cp.wait_send()
-    for q in (1, 2, 3):
-        stats[q].wait_recv()
+    for p in group:
+        rcopy(stat.at[0], stat.at[p], stat_ss.at[p], stat_rs.at[p], group[p]).wait_recv()
+    elsewhere = (
+        (((XP, 1), (XM, 1)), ((ZN, 2), (ZN, 2)), ((ZXP, 3), (ZXM, 3))),
+        (((XM, 0), (XP, 0)), ((ZXM, 2), (ZXP, 2)), ((ZN, 3), (ZN, 3))),
+        (((ZN, 0), (ZN, 0)), ((XP, 3), (XM, 3)), ((ZXP, 1), (ZXM, 1))),
+        (((ZXM, 0), (ZXP, 0)), ((XM, 2), (XP, 2)), ((ZN, 1), (ZN, 1))),
+    )
     for j in range(4):
-        m = [stat[q, (j ^ q) : (j ^ q) + 1, :] for q in range(4)]
-        s = [stat[q, 4 + (j ^ q) : 5 + (j ^ q), :] for q in range(4)]
+
+        def line(at, i):
+            return stat[at[0], i + at[1] : i + at[1] + 1, :]
+
+        m = [stat[0, j : j + 1, :]] + [halves(line(lo, 0), line(hi, 0)) for lo, hi in elsewhere[j]]
+        s = [stat[0, 4 + j : 5 + j, :]] + [halves(line(lo, 4), line(hi, 4)) for lo, hi in elsewhere[j]]
         top = jnp.maximum(jnp.maximum(m[0], m[1]), jnp.maximum(m[2], m[3]))
-        total = sum(s[q] * jnp.exp(m[q] - top) for q in range(4))
+        total = sum(s[i] * jnp.exp(m[i] - top) for i in range(4))
         log_total = top + jnp.log(total)
         if j == 0:
             logt_v[...] = log_total
             logt_out = pltpu.make_async_copy(logt_v, logt_hbm, o_sem.at[1])
             logt_out.start()
         cols = slice(RUN * j, RUN * (j + 1))
-        fac[:, cols] = meta[j, 0:1, :] * jnp.exp(mch[:, cols] - log_total)
-
-    def mass_step(i, carry):
-        f = fac[pl.ds(i, 1), :]
-        acc = jnp.zeros((PCH, RUN), F32)
+        fac[:, cols] = weights[j] * jnp.exp(mch[:, cols] - log_total)
+
+    for row, (scores, count) in enumerate(((scores_e, EARLY), (scores_l, LATE))):
+        acc = jnp.zeros((count, RUN), F32)
         for j in range(4):
-            acc = acc + scores[i, :, RUN * j : RUN * (j + 1)] * f[:, RUN * j : RUN * (j + 1)]
-        mp[i] = jnp.sum(acc.T, axis=0, keepdims=True)
-        return carry
-
-    lax.fori_loop(0, NPCH, mass_step, 0)
+            cols = slice(RUN * j, RUN * (j + 1))
+            acc = acc + scores[:, cols] * fac[row : row + 1, cols]
+        total = jnp.sum(acc.T, axis=0, keepdims=True)
+        at = slice(0, 768) if row == 0 else slice(768, 1024)
+        mp[0, :, at] = total[:, : count // 2]
+        mp[1, :, at] = total[:, count // 2 :]
 
     to_sib_mass = rcopy(mp.at[1], sib_in, m1_ss, m1_rs, sibling)
     to_sib_mass.start()
@@ -313,16 +372,10 @@
     for i in range(2 * DP):
         ms[i, :, :PART] = both[:, PART * i : PART * (i + 1)]
 
-    def mass_copy(line, to_line, dev):
-        rcopy(ms.at[line], mr.at[to_line], m2_ss, m2_rs, dev).start()
-
-    for r in range(4):
-        lo, hi = (d + r) % 4, 4 + (d + r) % 4
-        mass_copy(DP + lo, DP + d, (lo, cent_of(zhi, ym, k)))
-        mass_copy(DP + hi, DP + d, (hi, cent_of(zhi, yp, k)))
-    for r in range(1, DP):
-        mass_copy((d + r) % DP, d, row_peer(r))
-    own_mass = pltpu.make_async_copy(ms.at[d], mr.at[d], o_sem.at[2])
+    for i, o in enumerate(owners):
+        at, dev = owner(*o)
+        rcopy(ms.at[at], mr.at[i], m2_ss, m2_rs, dev).start()
+    own_mass = pltpu.make_async_copy(ms.at[owner(0, 0, 0)[0]], mr.at[2 * DP - 1], o_sem.at[2])
     own_mass.start()
     for cp in [to_sib_mass, *stats.values()]:
         cp.wait_send()
@@ -364,32 +417,33 @@
             pltpu.VMEM((DP, CAP, W), BF16),
             pltpu.VMEM((DP, 1, SLOTS), F32),
             pltpu.VMEM((DP, 1, SLOTS), F32),
-            pltpu.VMEM((NPCH * PCH, W), BF16),
+            pltpu.VMEM((EARLY + LATE, W), BF16),
             pltpu.VMEM((4, RUN, W), BF16),
-            pltpu.VMEM((4, 8, RUN), F32),
-            pltpu.VMEM((NPCH, PCH, 4 * RUN), F32),
-            pltpu.VMEM((NPCH, 4 * RUN), F32),
-            pltpu.VMEM((NPCH, 4 * RUN), F32),
-            pltpu.VMEM((4, 8, RUN), F32),
-            pltpu.VMEM((NPCH, 4 * RUN), F32),
-            pltpu.VMEM((NPCH, 1, PCH), F32),
-            pltpu.VMEM((1, PCH), F32),
+            pltpu.VMEM((6, 8, RUN), F32),
+            pltpu.VMEM((EARLY, 4 * RUN), F32),
+            pltpu.VMEM((LATE, 4 * RUN), F32),
+            pltpu.VMEM((2, 4 * RUN), F32),
+            pltpu.VMEM((2, 4 * RUN), F32),
+            pltpu.VMEM((6, 8, RUN), F32),
+            pltpu.VMEM((2, 4 * RUN), F32),
+            pltpu.VMEM((2, 1, 1024), F32),
+            pltpu.VMEM((1, 1024), F32),
             pltpu.VMEM((2 * DP, 1, RUN), F32),
             pltpu.VMEM((1, RUN), F32),
             dma((NTILE,)),
-            dma,
+            dma((2,)),
             dma((len(RANGES),)),
             dma((len(RANGES),)),
             dma,
             dma,
-            dma((5,)),
-            dma((5,)),
+            dma((12,)),
+            dma((12,)),
+            dma((10,)),
+            dma((10,)),
             dma((6,)),
             dma((6,)),
-            dma((3,)),
-            dma((3,)),
-            dma((3,)),
-            dma((3,)),
+            dma((6,)),
+            dma((6,)),
             dma,
             dma,
             dma,

time: 58.2 us -> 61.6 us (1.058)
  Pallas kernels: 57.4 us -> 60.8 us
    pallas_call x1, Pallas kernels: 56.6 us -> 60.1 us  [per_device(): pl.pallas_call(kernel, out_shape=(jax.ShapeDtypeStruct((RUN, W), BF16), j...]
where the time goes in v6:
time: 61.6 us; the launch traced here: 61.5 us
  Pallas kernels  60.8 us (99%)
  between operations  0.64 us (1%)
    pallas_call x1, Pallas kernels, per_device(): pl.pallas_call(kernel, out_shape=(jax.ShapeDtypeStruct((RUN, W), BF16), j...  60.1 us

profile of v6, /device:TPU:1, one launch (start us, length us, event | category | flops | bytes accessed | tf_op | source)
XLA Modules:
  0.0 61.5 jit_solution(7649952428663606290)
XLA Ops:
  0.6 60.1 %handover.1 = (bf16[128,1536]{1,0:T(8,128)(2,1)S(1)}, f32[1,128]{1,0:T(1,128)S(1)}, f32[16,1,128]{2,1,0:T(1,128)S(1)}) custom-call(s32[32,128]{1,0:T(8,128)} %bitcast.4, s32[1,128]{1,0:T(1,128)} %bitcast.5, bf16[4096,1536]{1,0:T(8,128)(2,1)} %e_hbm.1, bf16[512,1536]{1,0:T(8,128)(2,1)} %p_hbm.1), custom_call_target="tpu_custom_call" | custom-call | tf_op jit(solution)/shard_map/handover/pallas_call | solution.py:400
  60.7 0.8 %finish.1 = (bf16[128,1536]{1,0:T(8,128)(2,1)}, f32[1,128]{1,0:T(1,128)}, f32[1,64]{1,0:T(1,128)}) custom-call(bf16[128,1536]{1,0:T(8,128)(2,1)S(1)} %get-tuple-element.9.cent, f32[1,128]{1,0:T(1,128)S(1)} %get-tuple-element.10.logt, f32[16,1,128]{2,1,0:T(1,128)S(1)} %get-tuple-element.11.terms), custom_call_target="tpu_custom_call" | custom-call | tf_op jit(solution)/shard_map/finish/pallas_call | solution.py:459

commit v7 on v6

--- a/solution.py
+++ b/solution.py
@@ -21,6 +21,7 @@
 PART = 64
 EARLY, LATE = 1536, 512
 BLK = 128
+MCH = 512
 PIECES = (0, 2, 1, 3)
 INV_SOFT = 1.0 / 0.5
 REWARD = 1.5
@@ -32,7 +33,7 @@
 def kernel(
     a_hbm, label_hbm, e_hbm, p_hbm,
     cent_hbm, logt_hbm, mr,
-    a_v, label_v, e_v, oht, place, slot_v, send, recv, id_send, id_recv, par, cb, meta, scores_e, scores_l, mch, sch, stat, fac, mp, sib_in, ms, logt_v,
+    a_v, label_v, e_v, oht, place, slot_v, send, recv, id_send, id_recv, par, cb, meta, scores, mch, sch, stat, fac, terms, mp, sib_in, ms, logt_v,
     e_sem, p_sem, row_ss, row_rs, id_ss, id_rs, par_ss, par_rs, cb_ss, cb_rs, meta_ss, meta_rs, stat_ss, stat_rs,
     m1_ss, m1_rs, m2_ss, m2_rs, o_sem, in_sem,
 ):
@@ -247,9 +248,13 @@
     sib_early[0].start()
     to_down[0].wait_recv()
     sib_early[1].start()
-    for i in PIECES[:2]:
+    for i in PIECES:
         over_z[i].wait_recv()
         pass_on[i].start()
+    on_up.wait_recv()
+    sib_late[0].start()
+    on_down.wait_recv()
+    sib_late[1].start()
     for cp in own_par:
         cp.wait()
     for cp in (*to_sib, *over_x, *sib_early):
@@ -272,53 +277,54 @@
 
     weights, labels = meta_line(0), meta_line(1)
 
-    def first_ids(early):
-        found = []
-        for core in (k, 1 - k):
-            for t in (0, 1, 2) if early else (3,):
-                for a in range(2):
-                    found.append(cent_of(zhi, y_of[t], core) * SLAB + 2 * BLK * a + BLK * q)
-        return found
-
-    def score(pair, early):
+    firsts = [
+        cent_of(zhi, y_of[t], core) * SLAB + 2 * BLK * a + BLK * q
+        for times in ((0, 1, 2), (3,))
+        for core in (k, 1 - k)
+        for t in times
+        for a in range(2)
+    ]
+
+    def score(pair, size, first_step, steps):
         cols = slice(2 * RUN * pair, 2 * RUN * (pair + 1))
-        block = cb[2 * pair : 2 * pair + 2].reshape(2 * RUN, W)
         label = jnp.concatenate([labels[2 * pair], labels[2 * pair + 1]], axis=1).astype(jnp.int32)
-        some = par[:EARLY, :] if early else par[EARLY:, :]
-        s = lax.dot_general(some, block, (((1,), (1,)), ((), ())), preferred_element_type=F32)
-        line = lax.broadcasted_iota(jnp.int32, (BLK, 2 * RUN), 0)
-        s = jnp.concatenate(
-            [
-                s[BLK * i : BLK * (i + 1)] * INV_SOFT + jnp.where(line == label - first, REWARD, 0.0)
-                for i, first in enumerate(first_ids(early))
-            ],
-            axis=0,
-        )
-        top = jnp.max(s, axis=0, keepdims=True)
-        e = jnp.exp(s - top)
-        (scores_e if early else scores_l)[:, cols] = e
-        row = 0 if early else 1
-        mch[row : row + 1, cols] = top
-        sch[row : row + 1, cols] = jnp.sum(e, axis=0, keepdims=True)
-
-    score(0, True)
-    for i in PIECES[2:]:
-        over_z[i].wait_recv()
-        pass_on[i].start()
-    on_up.wait_recv()
-    sib_late[0].start()
-    on_down.wait_recv()
-    sib_late[1].start()
+        per = size // BLK
+
+        def step(i, carry):
+            rows = pl.ds(pl.multiple_of(i * size, size), size)
+            block = cb[2 * pair : 2 * pair + 2].reshape(2 * RUN, W)
+            s = lax.dot_general(par[rows, :], block, (((1,), (1,)), ((), ())), preferred_element_type=F32)
+            line = lax.broadcasted_iota(jnp.int32, (BLK, 2 * RUN), 0)
+            parts = []
+            for b in range(per):
+                first = firsts[per * first_step + b]
+                for other in range(first_step + 1, first_step + steps):
+                    first = jnp.where(i == other, firsts[per * other + b], first)
+                bonus = jnp.where(line == label - first, REWARD, 0.0)
+                parts.append(s[BLK * b : BLK * (b + 1)] * INV_SOFT + bonus)
+            s = jnp.concatenate(parts, axis=0)
+            top = jnp.max(s, axis=0, keepdims=True)
+            e = jnp.exp(s - top)
+            scores[rows, cols] = e
+            total = jnp.sum(e, axis=0, keepdims=True)
+            for h in range(size // MCH):
+                at = pl.ds(i * (size // MCH) + h, 1)
+                mch[at, cols] = top
+                sch[at, cols] = total if h == 0 else jnp.zeros_like(total)
+            return carry
+
+        lax.fori_loop(first_step, first_step + steps, step, 0)
+
+    score(0, MCH, 0, 3)
     for cp in (*to_up, *to_down, *to_sib, *sib_early, *metas.values(), *over_x):
         cp.wait_send()
     cent_out.wait()
     for cp in sib_late:
         cp.wait_recv()
-    score(0, False)
+    score(0, MCH, 3, 1)
     for cp in pass_on:
         cp.wait_recv()
-    score(1, True)
-    score(1, False)
+    score(1, 2 * MCH, 0, 2)
 
     m_loc = jnp.max(mch[...], axis=0, keepdims=True)
     s_loc = jnp.sum(sch[...] * jnp.exp(mch[...] - m_loc), axis=0, keepdims=True)
@@ -355,15 +361,23 @@
         cols = slice(RUN * j, RUN * (j + 1))
         fac[:, cols] = weights[j] * jnp.exp(mch[:, cols] - log_total)
 
-    for row, (scores, count) in enumerate(((scores_e, EARLY), (scores_l, LATE))):
-        acc = jnp.zeros((count, RUN), F32)
+    def mass_step(i, carry):
+        f = fac[pl.ds(i, 1), :]
+        rows = pl.ds(pl.multiple_of(i * MCH, MCH), MCH)
+        acc = jnp.zeros((MCH, RUN), F32)
         for j in range(4):
             cols = slice(RUN * j, RUN * (j + 1))
-            acc = acc + scores[:, cols] * fac[row : row + 1, cols]
-        total = jnp.sum(acc.T, axis=0, keepdims=True)
-        at = slice(0, 768) if row == 0 else slice(768, 1024)
-        mp[0, :, at] = total[:, : count // 2]
-        mp[1, :, at] = total[:, count // 2 :]
+            acc = acc + scores[rows, cols] * f[:, cols]
+        terms[i] = jnp.sum(acc.T, axis=0, keepdims=True)
+        return carry
+
+    lax.fori_loop(0, 4, mass_step, 0)
+    mp[0, :, 0:512] = terms[0]
+    mp[0, :, 512:768] = terms[1][:, :256]
+    mp[0, :, 768:1024] = terms[3][:, :256]
+    mp[1, :, 0:256] = terms[1][:, 256:]
+    mp[1, :, 256:768] = terms[2]
+    mp[1, :, 768:1024] = terms[3][:, 256:]
 
     to_sib_mass = rcopy(mp.at[1], sib_in, m1_ss, m1_rs, sibling)
     to_sib_mass.start()
@@ -420,12 +434,12 @@
             pltpu.VMEM((EARLY + LATE, W), BF16),
             pltpu.VMEM((4, RUN, W), BF16),
             pltpu.VMEM((6, 8, RUN), F32),
-            pltpu.VMEM((EARLY, 4 * RUN), F32),
-            pltpu.VMEM((LATE, 4 * RUN), F32),
-            pltpu.VMEM((2, 4 * RUN), F32),
-            pltpu.VMEM((2, 4 * RUN), F32),
+            pltpu.VMEM((EARLY + LATE, 4 * RUN), F32),
+            pltpu.VMEM((4, 4 * RUN), F32),
+            pltpu.VMEM((4, 4 * RUN), F32),
             pltpu.VMEM((6, 8, RUN), F32),
-            pltpu.VMEM((2, 4 * RUN), F32),
+            pltpu.VMEM((4, 4 * RUN), F32),
+            pltpu.VMEM((4, 1, MCH), F32),
             pltpu.VMEM((2, 1, 1024), F32),
             pltpu.VMEM((1, 1024), F32),
             pltpu.VMEM((2 * DP, 1, RUN), F32),

time: 61.6 us -> 58.6 us (0.951)
  Pallas kernels: 60.8 us -> 57.8 us
    pallas_call x1, Pallas kernels: 60.1 us -> 57.1 us  [per_device(): pl.pallas_call(kernel, out_shape=(jax.ShapeDtypeStruct((RUN, W), BF16), j...]
where the time goes in v7:
time: 58.6 us; the launch traced here: 58.5 us
  Pallas kernels  57.8 us (99%)
  between operations  0.64 us (1%)
    pallas_call x1, Pallas kernels, per_device(): pl.pallas_call(kernel, out_shape=(jax.ShapeDtypeStruct((RUN, W), BF16), j...  57.1 us

profile of v7, /device:TPU:1, one launch (start us, length us, event | category | flops | bytes accessed | tf_op | source)
XLA Modules:
  0.0 58.5 jit_solution(4378850347865750611)
XLA Ops:
  0.6 57.1 %handover.1 = (bf16[128,1536]{1,0:T(8,128)(2,1)S(1)}, f32[1,128]{1,0:T(1,128)S(1)}, f32[16,1,128]{2,1,0:T(1,128)S(1)}) custom-call(s32[32,128]{1,0:T(8,128)} %bitcast.4, s32[1,128]{1,0:T(1,128)} %bitcast.5, bf16[4096,1536]{1,0:T(8,128)(2,1)} %e_hbm.1, bf16[512,1536]{1,0:T(8,128)(2,1)} %p_hbm.1), custom_call_target="tpu_custom_call" | custom-call | tf_op jit(solution)/shard_map/handover/pallas_call | solution.py:414
  57.7 0.8 %finish.1 = (bf16[128,1536]{1,0:T(8,128)(2,1)}, f32[1,128]{1,0:T(1,128)}, f32[1,64]{1,0:T(1,128)}) custom-call(bf16[128,1536]{1,0:T(8,128)(2,1)S(1)} %get-tuple-element.9.cent, f32[1,128]{1,0:T(1,128)S(1)} %get-tuple-element.10.logt, f32[16,1,128]{2,1,0:T(1,128)S(1)} %get-tuple-element.11.terms), custom_call_target="tpu_custom_call" | custom-call | tf_op jit(solution)/shard_map/finish/pallas_call | solution.py:473

commit v8 on v7

--- a/solution.py
+++ b/solution.py
@@ -28,6 +28,7 @@
 
 RANGES = ((0, 256), (256, 512), (768, 768))
 SEND_AFTER = (0, 2, 5)
+FAR_FIRST = (5, 3, 4, 6, 2, 7, 1)
 
 
 def kernel(
@@ -148,6 +149,9 @@
 
     for cp in e_copies[2:]:
         cp.start()
+    pl.semaphore_wait(barrier, len(partners))
+    for cp in (to_up[0], to_down[1], to_up[1], to_down[0]):
+        cp.start()
 
     def row_copy(r, g, dev, owner):
         start, size = RANGES[g]
@@ -171,14 +175,9 @@
         e_copies[n].wait()
         part = jnp.dot(oht[...], e_v[n], preferred_element_type=F32)
         send[:, :, TILE * n : TILE * (n + 1)] = part.astype(BF16).reshape(DP, CAP, TILE)
-        if n == 0:
-            pl.semaphore_wait(barrier, len(partners))
         if n in SEND_AFTER:
-            for r in range(1, DP):
+            for r in FAR_FIRST:
                 row_copy(r, SEND_AFTER.index(n), row_peer(r), d).start()
-        if n == 0:
-            for cp in (to_up[0], to_down[1], to_up[1], to_down[0]):
-                cp.start()
         if n == 2:
             for cp in (*own_par, *to_sib):
                 cp.start()
@@ -197,6 +196,10 @@
     recv[d] = send[d]
     id_recv[d] = id_send[d]
     ms[...] = jnp.zeros_like(ms)
+    to_up[0].wait_recv()
+    on_up.start()
+    to_down[1].wait_recv()
+    on_down.start()
 
     id_total.wait_recv()
     ids = jnp.sum(id_recv[...], axis=0).astype(jnp.int32) - 1
@@ -237,10 +240,6 @@
     def arrived(p):
         return rcopy(meta.at[0], meta.at[p], meta_ss.at[p], meta_rs.at[p], group[p])
 
-    to_up[0].wait_recv()
-    on_up.start()
-    to_down[1].wait_recv()
-    on_down.start()
     for g in range(len(RANGES)):
         row_total(g).wait_send()
     id_total.wait_send()

time: 58.6 us -> 58.7 us (level)
  no operation moved by 1% of the time
where the time goes in v8:
time: 58.7 us; the launch traced here: 58.6 us
  Pallas kernels  57.9 us (99%)
  between operations  0.64 us (1%)
    pallas_call x1, Pallas kernels, per_device(): pl.pallas_call(kernel, out_shape=(jax.ShapeDtypeStruct((RUN, W), BF16), j...  57.2 us

profile of v8, /device:TPU:1, one launch (start us, length us, event | category | flops | bytes accessed | tf_op | source)
XLA Modules:
  0.0 58.6 jit_solution(12649787279462505826)
XLA Ops:
  0.6 57.2 %handover.1 = (bf16[128,1536]{1,0:T(8,128)(2,1)S(1)}, f32[1,128]{1,0:T(1,128)S(1)}, f32[16,1,128]{2,1,0:T(1,128)S(1)}) custom-call(s32[32,128]{1,0:T(8,128)} %bitcast.4, s32[1,128]{1,0:T(1,128)} %bitcast.5, bf16[4096,1536]{1,0:T(8,128)(2,1)} %e_hbm.1, bf16[512,1536]{1,0:T(8,128)(2,1)} %p_hbm.1), custom_call_target="tpu_custom_call" | custom-call | tf_op jit(solution)/shard_map/handover/pallas_call | solution.py:413
  57.8 0.8 %finish.1 = (bf16[128,1536]{1,0:T(8,128)(2,1)}, f32[1,128]{1,0:T(1,128)}, f32[1,64]{1,0:T(1,128)}) custom-call(bf16[128,1536]{1,0:T(8,128)(2,1)S(1)} %get-tuple-element.9.cent, f32[1,128]{1,0:T(1,128)S(1)} %get-tuple-element.10.logt, f32[16,1,128]{2,1,0:T(1,128)S(1)} %get-tuple-element.11.terms), custom_call_target="tpu_custom_call" | custom-call | tf_op jit(solution)/shard_map/finish/pallas_call | solution.py:472

commit v9 on v8

--- a/solution.py
+++ b/solution.py
@@ -15,7 +15,8 @@
 DP = 8
 SLOTS = DP * CAP
 TILE = 256
-NTILE = W // TILE
+COLS = W // 2
+NTILE = COLS // TILE
 ROWS = 4096
 SLAB = 512
 PART = 64
@@ -26,8 +27,8 @@
 INV_SOFT = 1.0 / 0.5
 REWARD = 1.5
 
-RANGES = ((0, 256), (256, 512), (768, 768))
-SEND_AFTER = (0, 2, 5)
+RANGES = ((0, 256), (256, 512))
+SEND_AFTER = (0, 2)
 FAR_FIRST = (5, 3, 4, 6, 2, 7, 1)
 
 
@@ -35,7 +36,7 @@
     a_hbm, label_hbm, e_hbm, p_hbm,
     cent_hbm, logt_hbm, mr,
     a_v, label_v, e_v, oht, place, slot_v, send, recv, id_send, id_recv, par, cb, meta, scores, mch, sch, stat, fac, terms, mp, sib_in, ms, logt_v,
-    e_sem, p_sem, row_ss, row_rs, id_ss, id_rs, par_ss, par_rs, cb_ss, cb_rs, meta_ss, meta_rs, stat_ss, stat_rs,
+    e_sem, p_sem, row_ss, row_rs, sib_ss, sib_rs, id_ss, id_rs, par_ss, par_rs, cb_ss, cb_rs, meta_ss, meta_rs, stat_ss, stat_rs,
     m1_ss, m1_rs, m2_ss, m2_rs, o_sem, in_sem,
 ):
     d = lax.axis_index("dp")
@@ -84,7 +85,10 @@
     load_a = pltpu.make_async_copy(a_hbm, a_v, in_sem.at[0])
     load_label = pltpu.make_async_copy(label_hbm, label_v, in_sem.at[1])
     e_copies = [
-        pltpu.make_async_copy(e_hbm.at[:, pl.ds(TILE * n, TILE)], e_v.at[n], e_sem.at[n]) for n in range(NTILE)
+        pltpu.make_async_copy(
+            e_hbm.at[:, pl.ds(pl.multiple_of(COLS * k + TILE * n, TILE), TILE)], e_v.at[n], e_sem.at[n]
+        )
+        for n in range(NTILE)
     ]
     def mine(a):
         return p_hbm.at[pl.ds(pl.multiple_of(2 * BLK * a + BLK * q, BLK), BLK)]
@@ -99,6 +103,7 @@
 
     barrier = pltpu.get_barrier_semaphore()
     partners = [row_peer(r) for r in range(1, DP)] + [group[ZN], group[ZXM], group[ZXP], sibling]
+    partners += [((d + r) % DP, cent_of(zhi, y, 1 - k)) for r in range(1, DP)]
     partners += [owner(*o)[1] for o in owners if o[0] != 0]
     for dev in partners:
         pl.semaphore_signal(barrier, inc=1, device_id=dev, device_id_type=MESH)
@@ -108,22 +113,23 @@
     load_a.wait()
 
     a = a_v[...]
-    rel = lax.shift_right_logical(a, 7) - c * DP
     run_id = lax.broadcasted_iota(jnp.int32, (32, 8, RUN), 1)
-    member = (rel[:, None, :] == run_id).astype(F32).reshape(256, RUN)
-    member_b = member.astype(BF16)
     upper = (
         lax.broadcasted_iota(jnp.int32, (RUN, RUN), 0) < lax.broadcasted_iota(jnp.int32, (RUN, RUN), 1)
     ).astype(F32).astype(BF16)
     ri = lax.broadcasted_iota(jnp.int32, (256, 256), 0)
     ci = lax.broadcasted_iota(jnp.int32, (256, 256), 1)
     before = (((ri & 7) == (ci & 7)) & (ci < ri)).astype(F32).astype(BF16)
-    within = jnp.dot(member_b, upper, preferred_element_type=F32)
-    earlier = jnp.dot(before, member_b, preferred_element_type=F32).astype(BF16)
-    ahead = jnp.dot(earlier, jnp.ones((RUN, RUN), BF16), preferred_element_type=F32)
     base = ((lax.broadcasted_iota(jnp.int32, (256, RUN), 0) & 7) * CAP + 1).astype(F32)
-    slot = jnp.sum((member * (within + ahead + base)).reshape(32, 8, RUN), axis=1) - 1.0
-    slot_v[...] = slot.astype(jnp.int32)
+    for stage in range(2):
+        rel = lax.shift_right_logical(a, 7) - cent_of(zhi, y, stage) * DP
+        member = (rel[:, None, :] == run_id).astype(F32).reshape(256, RUN)
+        member_b = member.astype(BF16)
+        within = jnp.dot(member_b, upper, preferred_element_type=F32)
+        earlier = jnp.dot(before, member_b, preferred_element_type=F32).astype(BF16)
+        ahead = jnp.dot(earlier, jnp.ones((RUN, RUN), BF16), preferred_element_type=F32)
+        slot = jnp.sum((member * (within + ahead + base)).reshape(32, 8, RUN), axis=1) - 1.0
+        slot_v[stage] = slot.astype(jnp.int32)
     spot = ((a & (RUN - 1)) + 1).astype(F32)
     for b in range(ROWS // RUN):
         place[:, RUN * b : RUN * (b + 1)] = jnp.broadcast_to(spot[b : b + 1, :], (16, RUN)).astype(BF16)
@@ -139,13 +145,16 @@
     sib_early = [par_copy(place_of(0, t, 0, 2), place_of(1, t, 0, 2), 7 + t, sibling) for t in (1, 2)]
     sib_late = [par_copy(place_of(0, 3, a), place_of(1, 3, a), 10 + a, sibling) for a in range(2)]
 
-    def build(b, carry):
-        cols = pl.ds(pl.multiple_of(b * RUN, RUN), RUN)
-        line = slot_v[pl.ds(b, 1), :]
-        oht[:, cols] = (lax.broadcasted_iota(jnp.int32, (SLOTS, RUN), 0) == line).astype(F32).astype(BF16)
-        return carry
-
-    lax.fori_loop(0, ROWS // RUN, build, 0)
+    def build(stage):
+        def block(b, carry):
+            cols = pl.ds(pl.multiple_of(b * RUN, RUN), RUN)
+            line = slot_v[stage, pl.ds(b, 1), :]
+            oht[stage, :, cols] = (lax.broadcasted_iota(jnp.int32, (SLOTS, RUN), 0) == line).astype(F32).astype(BF16)
+            return carry
+
+        lax.fori_loop(0, ROWS // RUN, block, 0)
+
+    build(0)
 
     for cp in e_copies[2:]:
         cp.start()
@@ -153,47 +162,53 @@
     for cp in (to_up[0], to_down[1], to_up[1], to_down[0]):
         cp.start()
 
-    def row_copy(r, g, dev, owner):
+    def there(start, size):
+        return pl.ds(pl.multiple_of(COLS * k + start, TILE), size)
+
+    def row_copy(r, stage, g):
         start, size = RANGES[g]
+        to = (d + r) % DP
         return rcopy(
-            send.at[dev[0], :, pl.ds(start, size)],
-            recv.at[owner, :, pl.ds(start, size)],
-            row_ss.at[g],
-            row_rs.at[g],
-            dev,
+            send.at[stage, to, :, pl.ds(start, size)],
+            recv.at[d, :, there(start, size)],
+            row_ss.at[stage],
+            row_rs,
+            (to, cent_of(zhi, y, stage)),
         )
 
-    def row_total(g):
-        start, size = RANGES[g]
-        cols = pl.ds(start, size)
-        part = pl.ds(0, DP - 1)
-        return rcopy(send.at[part, :, cols], recv.at[part, :, cols], row_ss.at[g], row_rs.at[g], row_peer(1))
-
-    id_total = rcopy(id_send.at[pl.ds(0, DP - 1)], id_recv.at[pl.ds(0, DP - 1)], id_ss, id_rs, row_peer(1))
-
-    for n in range(NTILE):
-        e_copies[n].wait()
-        part = jnp.dot(oht[...], e_v[n], preferred_element_type=F32)
-        send[:, :, TILE * n : TILE * (n + 1)] = part.astype(BF16).reshape(DP, CAP, TILE)
-        if n in SEND_AFTER:
-            for r in FAR_FIRST:
-                row_copy(r, SEND_AFTER.index(n), row_peer(r), d).start()
-        if n == 2:
+    peers = pl.ds(0, DP - 1)
+    rows_in = rcopy(recv.at[peers], recv.at[peers], row_ss.at[0], row_rs, row_peer(1))
+    rows_out = [rcopy(send.at[i, peers], send.at[i, peers], row_ss.at[i], row_rs, row_peer(1)) for i in range(2)]
+    rows_sib = rcopy(send.at[1 - k, d], recv.at[d, :, there(0, COLS)], sib_ss, sib_rs, sibling)
+    id_total = rcopy(id_send.at[peers], id_recv.at[peers], id_ss, id_rs, row_peer(1))
+
+    for stage in range(2):
+        for n in range(NTILE):
+            if stage == 0:
+                e_copies[n].wait()
+            part = jnp.dot(oht[stage], e_v[n], preferred_element_type=F32)
+            send[stage, :, :, TILE * n : TILE * (n + 1)] = part.astype(BF16).reshape(DP, CAP, TILE)
+            if n in SEND_AFTER:
+                for r in FAR_FIRST:
+                    row_copy(r, stage, SEND_AFTER.index(n)).start()
+        if stage == 0:
             for cp in (*own_par, *to_sib):
                 cp.start()
-            spots = lax.dot_general(place[...], oht[...], (((1,), (1,)), ((), ())), preferred_element_type=F32)[:8]
+            build(1)
+            spots = lax.dot_general(place[...], oht[k], (((1,), (1,)), ((), ())), preferred_element_type=F32)[:8]
             lane = lax.broadcasted_iota(jnp.int32, (DP, SLOTS), 1)
-            mine = jnp.where(lane // CAP == lax.broadcasted_iota(jnp.int32, (DP, SLOTS), 0), spots, 0.0).astype(BF16)
+            mine_at = jnp.where(lane // CAP == lax.broadcasted_iota(jnp.int32, (DP, SLOTS), 0), spots, 0.0).astype(BF16)
             lo = lax.broadcasted_iota(jnp.int32, (SLOTS, SLOTS), 0)
             hi = lax.broadcasted_iota(jnp.int32, (SLOTS, SLOTS), 1)
             shift = ((lo % CAP == hi % CAP) & (hi // CAP == d)).astype(F32).astype(BF16)
-            moved = jnp.dot(mine, shift, preferred_element_type=F32)
+            moved = jnp.dot(mine_at, shift, preferred_element_type=F32)
             for i in range(DP):
                 id_send[i] = moved[i : i + 1, :]
-            for r in range(1, DP):
+            for r in FAR_FIRST:
                 dev = row_peer(r)
                 rcopy(id_send.at[dev[0]], id_recv.at[d], id_ss, id_rs, dev).start()
-    recv[d] = send[d]
+    rows_sib.start()
+    recv[d, :, there(0, COLS)] = send[k, d]
     id_recv[d] = id_send[d]
     ms[...] = jnp.zeros_like(ms)
     to_up[0].wait_recv()
@@ -207,8 +222,8 @@
     counts_col = jnp.sum(onehot, axis=1, keepdims=True)
     onehot = onehot.astype(BF16)
     counts_row = lax.dot_general(jnp.ones((16, SLOTS), BF16), onehot, (((1,), (1,)), ((), ())), preferred_element_type=F32)[:1]
-    for g in range(len(RANGES)):
-        row_total(g).wait_recv()
+    rows_in.wait_recv()
+    rows_sib.wait_recv()
     sums = jnp.dot(onehot, recv[...].reshape(SLOTS, W), preferred_element_type=F32)
     mean = sums / jnp.maximum(counts_col, 1.0)
     scale = jnp.sqrt(jnp.sum(mean * mean, axis=1, keepdims=True) + 1e-06)
@@ -240,8 +255,8 @@
     def arrived(p):
         return rcopy(meta.at[0], meta.at[p], meta_ss.at[p], meta_rs.at[p], group[p])
 
-    for g in range(len(RANGES)):
-        row_total(g).wait_send()
+    for cp in (*rows_out, rows_sib):
+        cp.wait_send()
     id_total.wait_send()
     to_up[1].wait_recv()
     sib_early[0].start()
@@ -423,10 +438,10 @@
             pltpu.VMEM((32, RUN), jnp.int32),
             pltpu.VMEM((1, RUN), jnp.int32),
             pltpu.VMEM((NTILE, ROWS, TILE), BF16),
-            pltpu.VMEM((SLOTS, ROWS), BF16),
+            pltpu.VMEM((2, SLOTS, ROWS), BF16),
             pltpu.VMEM((16, ROWS), BF16),
-            pltpu.VMEM((32, RUN), jnp.int32),
-            pltpu.VMEM((DP, CAP, W), BF16),
+            pltpu.VMEM((2, 32, RUN), jnp.int32),
+            pltpu.VMEM((2, DP, CAP, COLS), BF16),
             pltpu.VMEM((DP, CAP, W), BF16),
             pltpu.VMEM((DP, 1, SLOTS), F32),
             pltpu.VMEM((DP, 1, SLOTS), F32),
@@ -445,8 +460,10 @@
             pltpu.VMEM((1, RUN), F32),
             dma((NTILE,)),
             dma((2,)),
-            dma((len(RANGES),)),
-            dma((len(RANGES),)),
+            dma((2,)),
+            dma,
+            dma,
+            dma,
             dma,
             dma,
             dma((12,)),

time: 58.7 us -> 54.1 us (0.922)
  Pallas kernels: 57.9 us -> 53.3 us
    pallas_call x1, Pallas kernels: 57.2 us -> 52.5 us  [per_device(): pl.pallas_call(kernel, out_shape=(jax.ShapeDtypeStruct((RUN, W), BF16), j...]
where the time goes in v9:
time: 54.1 us; the launch traced here: 53.9 us
  Pallas kernels  53.3 us (99%)
  between operations  0.64 us (1%)
    pallas_call x1, Pallas kernels, per_device(): pl.pallas_call(kernel, out_shape=(jax.ShapeDtypeStruct((RUN, W), BF16), j...  52.5 us

profile of v9, /device:TPU:1, one launch (start us, length us, event | category | flops | bytes accessed | tf_op | source)
XLA Modules:
  0.0 53.9 jit_solution(11632872165753745200)
XLA Ops:
  0.6 52.5 %handover.1 = (bf16[128,1536]{1,0:T(8,128)(2,1)S(1)}, f32[1,128]{1,0:T(1,128)S(1)}, f32[16,1,128]{2,1,0:T(1,128)S(1)}) custom-call(s32[32,128]{1,0:T(8,128)} %bitcast.4, s32[1,128]{1,0:T(1,128)} %bitcast.5, bf16[4096,1536]{1,0:T(8,128)(2,1)} %e_hbm.1, bf16[512,1536]{1,0:T(8,128)(2,1)} %p_hbm.1), custom_call_target="tpu_custom_call" | custom-call | tf_op jit(solution)/shard_map/handover/pallas_call | solution.py:428
  53.2 0.8 %finish.1 = (bf16[128,1536]{1,0:T(8,128)(2,1)}, f32[1,128]{1,0:T(1,128)}, f32[1,64]{1,0:T(1,128)}) custom-call(bf16[128,1536]{1,0:T(8,128)(2,1)S(1)} %get-tuple-element.9.cent, f32[1,128]{1,0:T(1,128)S(1)} %get-tuple-element.10.logt, f32[16,1,128]{2,1,0:T(1,128)S(1)} %get-tuple-element.11.terms), custom_call_target="tpu_custom_call" | custom-call | tf_op jit(solution)/shard_map/finish/pallas_call | solution.py:489

commit v10 on v9

--- a/solution.py
+++ b/solution.py
@@ -121,7 +121,7 @@
     ci = lax.broadcasted_iota(jnp.int32, (256, 256), 1)
     before = (((ri & 7) == (ci & 7)) & (ci < ri)).astype(F32).astype(BF16)
     base = ((lax.broadcasted_iota(jnp.int32, (256, RUN), 0) & 7) * CAP + 1).astype(F32)
-    for stage in range(2):
+    def find_slots(stage):
         rel = lax.shift_right_logical(a, 7) - cent_of(zhi, y, stage) * DP
         member = (rel[:, None, :] == run_id).astype(F32).reshape(256, RUN)
         member_b = member.astype(BF16)
@@ -130,9 +130,8 @@
         ahead = jnp.dot(earlier, jnp.ones((RUN, RUN), BF16), preferred_element_type=F32)
         slot = jnp.sum((member * (within + ahead + base)).reshape(32, 8, RUN), axis=1) - 1.0
         slot_v[stage] = slot.astype(jnp.int32)
-    spot = ((a & (RUN - 1)) + 1).astype(F32)
-    for b in range(ROWS // RUN):
-        place[:, RUN * b : RUN * (b + 1)] = jnp.broadcast_to(spot[b : b + 1, :], (16, RUN)).astype(BF16)
+
+    find_slots(0)
 
     def par_copy(src, dst, idx, dev):
         return rcopy(src, dst, par_ss.at[idx], par_rs.at[idx], dev)
@@ -154,12 +153,12 @@
 
         lax.fori_loop(0, ROWS // RUN, block, 0)
 
-    build(0)
-
-    for cp in e_copies[2:]:
-        cp.start()
     pl.semaphore_wait(barrier, len(partners))
     for cp in (to_up[0], to_down[1], to_up[1], to_down[0]):
+        cp.start()
+    build(0)
+
+    for cp in e_copies[2:]:
         cp.start()
 
     def there(start, size):
@@ -194,7 +193,11 @@
         if stage == 0:
             for cp in (*own_par, *to_sib):
                 cp.start()
+            find_slots(1)
             build(1)
+            spot = ((a & (RUN - 1)) + 1).astype(F32)
+            for b in range(ROWS // RUN):
+                place[:, RUN * b : RUN * (b + 1)] = jnp.broadcast_to(spot[b : b + 1, :], (16, RUN)).astype(BF16)
             spots = lax.dot_general(place[...], oht[k], (((1,), (1,)), ((), ())), preferred_element_type=F32)[:8]
             lane = lax.broadcasted_iota(jnp.int32, (DP, SLOTS), 1)
             mine_at = jnp.where(lane // CAP == lax.broadcasted_iota(jnp.int32, (DP, SLOTS), 0), spots, 0.0).astype(BF16)

time: 54.1 us -> 54.1 us (level)
  no operation moved by 1% of the time
where the time goes in v10:
time: 54.1 us; the launch traced here: 53.9 us
  Pallas kernels  53.3 us (99%)
  between operations  0.64 us (1%)
    pallas_call x1, Pallas kernels, per_device(): pl.pallas_call(kernel, out_shape=(jax.ShapeDtypeStruct((RUN, W), BF16), j...  52.5 us

profile of v10, /device:TPU:1, one launch (start us, length us, event | category | flops | bytes accessed | tf_op | source)
XLA Modules:
  0.0 53.9 jit_solution(8945961213149207774)
XLA Ops:
  0.6 52.5 %handover.1 = (bf16[128,1536]{1,0:T(8,128)(2,1)S(1)}, f32[1,128]{1,0:T(1,128)S(1)}, f32[16,1,128]{2,1,0:T(1,128)S(1)}) custom-call(s32[32,128]{1,0:T(8,128)} %bitcast.4, s32[1,128]{1,0:T(1,128)} %bitcast.5, bf16[4096,1536]{1,0:T(8,128)(2,1)} %e_hbm.1, bf16[512,1536]{1,0:T(8,128)(2,1)} %p_hbm.1), custom_call_target="tpu_custom_call" | custom-call | tf_op jit(solution)/shard_map/handover/pallas_call | solution.py:431
  53.1 0.8 %finish.1 = (bf16[128,1536]{1,0:T(8,128)(2,1)}, f32[1,128]{1,0:T(1,128)}, f32[1,64]{1,0:T(1,128)}) custom-call(bf16[128,1536]{1,0:T(8,128)(2,1)S(1)} %get-tuple-element.9.cent, f32[1,128]{1,0:T(1,128)S(1)} %get-tuple-element.10.logt, f32[16,1,128]{2,1,0:T(1,128)S(1)} %get-tuple-element.11.terms), custom_call_target="tpu_custom_call" | custom-call | tf_op jit(solution)/shard_map/finish/pallas_call | solution.py:492

commit v11 on v9

--- a/solution.py
+++ b/solution.py
@@ -265,10 +265,6 @@
     for i in PIECES:
         over_z[i].wait_recv()
         pass_on[i].start()
-    on_up.wait_recv()
-    sib_late[0].start()
-    on_down.wait_recv()
-    sib_late[1].start()
     for cp in own_par:
         cp.wait()
     for cp in (*to_sib, *over_x, *sib_early):
@@ -329,16 +325,23 @@
 
         lax.fori_loop(first_step, first_step + steps, step, 0)
 
-    score(0, MCH, 0, 3)
+    score(0, 2 * MCH, 0, 1)
+    score(0, MCH, 2, 1)
+    on_up.wait_recv()
+    sib_late[0].start()
+    on_down.wait_recv()
+    sib_late[1].start()
+    for cp in pass_on:
+        cp.wait_recv()
+    score(1, 2 * MCH, 0, 1)
+    score(1, MCH, 2, 1)
     for cp in (*to_up, *to_down, *to_sib, *sib_early, *metas.values(), *over_x):
         cp.wait_send()
     cent_out.wait()
     for cp in sib_late:
         cp.wait_recv()
     score(0, MCH, 3, 1)
-    for cp in pass_on:
-        cp.wait_recv()
-    score(1, 2 * MCH, 0, 2)
+    score(1, MCH, 3, 1)
 
     m_loc = jnp.max(mch[...], axis=0, keepdims=True)
     s_loc = jnp.sum(sch[...] * jnp.exp(mch[...] - m_loc), axis=0, keepdims=True)

time: 54.1 us -> 52 us (0.961)
  Pallas kernels: 53.3 us -> 51.2 us
    pallas_call x1, Pallas kernels: 52.5 us -> 50.4 us  [per_device(): pl.pallas_call(kernel, out_shape=(jax.ShapeDtypeStruct((RUN, W), BF16), j...]
where the time goes in v11:
time: 52 us; the launch traced here: 51.8 us
  Pallas kernels  51.2 us (98%)
  between operations  0.64 us (1%)
    pallas_call x1, Pallas kernels, per_device(): pl.pallas_call(kernel, out_shape=(jax.ShapeDtypeStruct((RUN, W), BF16), j...  50.4 us

profile of v11, /device:TPU:1, one launch (start us, length us, event | category | flops | bytes accessed | tf_op | source)
XLA Modules:
  0.0 51.8 jit_solution(16105409668970659441)
XLA Ops:
  0.6 50.4 %handover.1 = (bf16[128,1536]{1,0:T(8,128)(2,1)S(1)}, f32[1,128]{1,0:T(1,128)S(1)}, f32[16,1,128]{2,1,0:T(1,128)S(1)}) custom-call(s32[32,128]{1,0:T(8,128)} %bitcast.4, s32[1,128]{1,0:T(1,128)} %bitcast.5, bf16[4096,1536]{1,0:T(8,128)(2,1)} %e_hbm.1, bf16[512,1536]{1,0:T(8,128)(2,1)} %p_hbm.1), custom_call_target="tpu_custom_call" | custom-call | tf_op jit(solution)/shard_map/handover/pallas_call | solution.py:431
  51.0 0.8 %finish.1 = (bf16[128,1536]{1,0:T(8,128)(2,1)}, f32[1,128]{1,0:T(1,128)}, f32[1,64]{1,0:T(1,128)}) custom-call(bf16[128,1536]{1,0:T(8,128)(2,1)S(1)} %get-tuple-element.9.cent, f32[1,128]{1,0:T(1,128)S(1)} %get-tuple-element.10.logt, f32[16,1,128]{2,1,0:T(1,128)S(1)} %get-tuple-element.11.terms), custom_call_target="tpu_custom_call" | custom-call | tf_op jit(solution)/shard_map/finish/pallas_call | solution.py:492

commit v12 on v11

--- a/solution.py
+++ b/solution.py
@@ -121,7 +121,7 @@
     ci = lax.broadcasted_iota(jnp.int32, (256, 256), 1)
     before = (((ri & 7) == (ci & 7)) & (ci < ri)).astype(F32).astype(BF16)
     base = ((lax.broadcasted_iota(jnp.int32, (256, RUN), 0) & 7) * CAP + 1).astype(F32)
-    for stage in range(2):
+    def find_slots(stage):
         rel = lax.shift_right_logical(a, 7) - cent_of(zhi, y, stage) * DP
         member = (rel[:, None, :] == run_id).astype(F32).reshape(256, RUN)
         member_b = member.astype(BF16)
@@ -130,9 +130,8 @@
         ahead = jnp.dot(earlier, jnp.ones((RUN, RUN), BF16), preferred_element_type=F32)
         slot = jnp.sum((member * (within + ahead + base)).reshape(32, 8, RUN), axis=1) - 1.0
         slot_v[stage] = slot.astype(jnp.int32)
-    spot = ((a & (RUN - 1)) + 1).astype(F32)
-    for b in range(ROWS // RUN):
-        place[:, RUN * b : RUN * (b + 1)] = jnp.broadcast_to(spot[b : b + 1, :], (16, RUN)).astype(BF16)
+
+    find_slots(0)
 
     def par_copy(src, dst, idx, dev):
         return rcopy(src, dst, par_ss.at[idx], par_rs.at[idx], dev)
@@ -154,12 +153,12 @@
 
         lax.fori_loop(0, ROWS // RUN, block, 0)
 
-    build(0)
-
-    for cp in e_copies[2:]:
-        cp.start()
     pl.semaphore_wait(barrier, len(partners))
     for cp in (to_up[0], to_down[1], to_up[1], to_down[0]):
+        cp.start()
+    build(0)
+
+    for cp in e_copies[2:]:
         cp.start()
 
     def there(start, size):
@@ -194,7 +193,11 @@
         if stage == 0:
             for cp in (*own_par, *to_sib):
                 cp.start()
+            find_slots(1)
             build(1)
+            spot = ((a & (RUN - 1)) + 1).astype(F32)
+            for b in range(ROWS // RUN):
+                place[:, RUN * b : RUN * (b + 1)] = jnp.broadcast_to(spot[b : b + 1, :], (16, RUN)).astype(BF16)
             spots = lax.dot_general(place[...], oht[k], (((1,), (1,)), ((), ())), preferred_element_type=F32)[:8]
             lane = lax.broadcasted_iota(jnp.int32, (DP, SLOTS), 1)
             mine_at = jnp.where(lane // CAP == lax.broadcasted_iota(jnp.int32, (DP, SLOTS), 0), spots, 0.0).astype(BF16)

time: 52 us -> 53.1 us (1.021)
  Pallas kernels: 51.2 us -> 52.3 us
    pallas_call x1, Pallas kernels: 50.4 us -> 51.5 us  [per_device(): pl.pallas_call(kernel, out_shape=(jax.ShapeDtypeStruct((RUN, W), BF16), j...]
where the time goes in v12:
time: 53.1 us; the launch traced here: 52.9 us
  Pallas kernels  52.3 us (98%)
  between operations  0.64 us (1%)
    pallas_call x1, Pallas kernels, per_device(): pl.pallas_call(kernel, out_shape=(jax.ShapeDtypeStruct((RUN, W), BF16), j...  51.5 us

profile of v12, /device:TPU:1, one launch (start us, length us, event | category | flops | bytes accessed | tf_op | source)
XLA Modules:
  0.0 52.9 jit_solution(15959418927485661061)
XLA Ops:
  0.6 51.5 %handover.1 = (bf16[128,1536]{1,0:T(8,128)(2,1)S(1)}, f32[1,128]{1,0:T(1,128)S(1)}, f32[16,1,128]{2,1,0:T(1,128)S(1)}) custom-call(s32[32,128]{1,0:T(8,128)} %bitcast.4, s32[1,128]{1,0:T(1,128)} %bitcast.5, bf16[4096,1536]{1,0:T(8,128)(2,1)} %e_hbm.1, bf16[512,1536]{1,0:T(8,128)(2,1)} %p_hbm.1), custom_call_target="tpu_custom_call" | custom-call | tf_op jit(solution)/shard_map/handover/pallas_call | solution.py:434
  52.1 0.8 %finish.1 = (bf16[128,1536]{1,0:T(8,128)(2,1)}, f32[1,128]{1,0:T(1,128)}, f32[1,64]{1,0:T(1,128)}) custom-call(bf16[128,1536]{1,0:T(8,128)(2,1)S(1)} %get-tuple-element.9.cent, f32[1,128]{1,0:T(1,128)S(1)} %get-tuple-element.10.logt, f32[16,1,128]{2,1,0:T(1,128)S(1)} %get-tuple-element.11.terms), custom_call_target="tpu_custom_call" | custom-call | tf_op jit(solution)/shard_map/finish/pallas_call | solution.py:495

commit v13 on v11

--- a/solution.py
+++ b/solution.py
@@ -335,9 +335,6 @@
         cp.wait_recv()
     score(1, 2 * MCH, 0, 1)
     score(1, MCH, 2, 1)
-    for cp in (*to_up, *to_down, *to_sib, *sib_early, *metas.values(), *over_x):
-        cp.wait_send()
-    cent_out.wait()
     for cp in sib_late:
         cp.wait_recv()
     score(0, MCH, 3, 1)
@@ -351,6 +348,9 @@
     stats = {p: rcopy(stat.at[0], stat.at[inverse[p]], stat_ss.at[p], stat_rs.at[inverse[p]], group[p]) for p in group}
     for p in (ZXM, ZXP, ZN, XM, XP):
         stats[p].start()
+    for cp in (*to_up, *to_down, *to_sib, *sib_early, *metas.values(), *over_x):
+        cp.wait_send()
+    cent_out.wait()
     for cp in (*over_z, *pass_on, on_up, on_down, *sib_late):
         cp.wait_send()
     for p in group:

time: 52 us -> 52 us (level)
  no operation moved by 1% of the time
where the time goes in v13:
time: 52 us; the launch traced here: 51.8 us
  Pallas kernels  51.2 us (98%)
  between operations  0.64 us (1%)
    pallas_call x1, Pallas kernels, per_device(): pl.pallas_call(kernel, out_shape=(jax.ShapeDtypeStruct((RUN, W), BF16), j...  50.4 us

profile of v13, /device:TPU:1, one launch (start us, length us, event | category | flops | bytes accessed | tf_op | source)
XLA Modules:
  0.0 51.8 jit_solution(7127226756273728798)
XLA Ops:
  0.6 50.4 %handover.1 = (bf16[128,1536]{1,0:T(8,128)(2,1)S(1)}, f32[1,128]{1,0:T(1,128)S(1)}, f32[16,1,128]{2,1,0:T(1,128)S(1)}) custom-call(s32[32,128]{1,0:T(8,128)} %bitcast.4, s32[1,128]{1,0:T(1,128)} %bitcast.5, bf16[4096,1536]{1,0:T(8,128)(2,1)} %e_hbm.1, bf16[512,1536]{1,0:T(8,128)(2,1)} %p_hbm.1), custom_call_target="tpu_custom_call" | custom-call | tf_op jit(solution)/shard_map/handover/pallas_call | solution.py:431
  51.0 0.8 %finish.1 = (bf16[128,1536]{1,0:T(8,128)(2,1)}, f32[1,128]{1,0:T(1,128)}, f32[1,64]{1,0:T(1,128)}) custom-call(bf16[128,1536]{1,0:T(8,128)(2,1)S(1)} %get-tuple-element.9.cent, f32[1,128]{1,0:T(1,128)S(1)} %get-tuple-element.10.logt, f32[16,1,128]{2,1,0:T(1,128)S(1)} %get-tuple-element.11.terms), custom_call_target="tpu_custom_call" | custom-call | tf_op jit(solution)/shard_map/finish/pallas_call | solution.py:492
